TPU v7x, 512 devices: a whole 4x4x16 slice. The times are simulated.
512 devices in a mesh: dp: 32 (over z, x_hi), tensor: 16 (over y, x_lo, core).
Axes of the slice: x: 4 (x_hi: 2, x_lo: 2; x = x_hi * 2 + x_lo), y: 4, z: 16, core: 2. Of those that a mesh axis runs over, the one named last changes fastest.
Arguments:
- hidden: bfloat16 [4096, 4096], P(('dp', 'tensor')), parts along dimension 0, may hold values from -6 to 6
- in_weight: bfloat16 [4096, 6208], P('tensor'), may hold values from -0.09375 to 0.09375
- out_weight: bfloat16 [2048, 4096], P(None, 'tensor'), may hold values from -0.125 to 0.125
- conv_weight: float32 [4, 4096], replicated, may hold values from -3 to 3
- head_params: float32 [3, 64], replicated, may hold values from -5.3 to 1.5, as said below
- packing: int32 [5], replicated, may hold values from 0 to 4, each once
- head_group: int32 [64], replicated, may hold values from 0 to 7, as said below
Outputs:
- layer_out: bfloat16 [4096, 4096], P(('dp', 'tensor')), parts along dimension 0
There are 32 independent parts, one for each index of `dp`. A program takes and returns all parts, laid end to end along the dimension named above; an argument that names none is the same for every part. Nothing has to cross between parts.
Inputs may be any that keep to these rules, and one draw needn't show every extreme that they name: `packing`: each segment is named once. `head_group`: each group holds exactly 8 heads. `head_params`: row 0 lies in -4 to -1, row 1 holds logarithms of decay rates, row 2 lies in 0.5 to 1.5.
All inputs are finite; a program needn't handle non-finite values.
Results may differ from a plain program's by a relative error of at most 0.023.
Values may be sent and summed in bfloat16 or wider, within the bound.
No kernel may reach another device: no remote copies, remote signals or barrier semaphores. Data moves between devices by JAX's collectives and lax.ppermute only.
A program may use at most 64 MiB of HBM per device.

v0:
```python
import jax
import jax.numpy as jnp
from jax import lax
from jax.sharding import PartitionSpec as P

D = 4096
HEADS = 64
HEAD_DIM = 32
GROUPS = 8
STATE = 128
SEQ = 128


epsilon = 1e-05


def segment_offsets(packing, widths):
    width_table = jnp.array(widths, dtype=jnp.int32)
    placed = jnp.take(width_table, packing)
    starts = jnp.cumsum(placed) - placed
    return [jnp.sum(jnp.where(packing == number, starts, 0)) for number in range(5)]


def causal_conv(values, conv_taps):
    length = values.shape[0]
    kernel = conv_taps.shape[0]
    padded = jnp.pad(values.astype(jnp.float32), ((kernel - 1, 0), (0, 0)))
    summed = jnp.zeros(values.shape, jnp.float32)
    for offset in range(kernel):
        summed = summed + conv_taps[offset] * padded[offset : offset + length]
    return jax.nn.silu(summed).astype(jnp.bfloat16)


def state_mixing(x_heads, b_heads, c_heads, step_size, cumulative):
    length = x_heads.shape[0]
    scores = jnp.einsum("thn,shn->hts", c_heads, b_heads, precision=lax.Precision.HIGHEST)
    positions = jnp.arange(length)
    causal = positions[:, None] >= positions[None, :]
    spread = cumulative.T[:, :, None] - cumulative.T[:, None, :]
    weights = jnp.where(causal[None], jnp.exp(jnp.where(causal[None], spread, 0.0)), 0.0)
    weights = weights * scores * step_size.T[:, None, :]
    return jnp.einsum("hts,shp->thp", weights, x_heads, precision=lax.Precision.HIGHEST)


def gated_heads(gate_raw, x_values, b_full, c_full, dt_raw, params, member):
    length = x_values.shape[0]
    head_count = member.shape[0]
    x_heads = x_values.astype(jnp.float32).reshape(length, head_count, -1)
    b_heads = jnp.einsum("lgn,hg->lhn", b_full, member, precision=lax.Precision.HIGHEST)
    c_heads = jnp.einsum("lgn,hg->lhn", c_full, member, precision=lax.Precision.HIGHEST)
    step_size = jax.nn.softplus(dt_raw.astype(jnp.float32) + params[0][None, :])
    cumulative = jnp.cumsum(-step_size * jnp.exp(params[1])[None, :], axis=0)
    mixed = state_mixing(x_heads, b_heads, c_heads, step_size, cumulative)
    mixed = mixed + params[2][None, :, None] * x_heads
    gate_act = jax.nn.silu(gate_raw.astype(jnp.float32)).reshape(length, head_count, -1)
    return mixed * gate_act


def shards(hidden, in_weight, out_weight, conv_weight, head_params, packing, head_group):
    group_size = lax.axis_size("tensor")
    my_index = lax.axis_index("tensor")
    inner = HEADS * HEAD_DIM
    width_bc = GROUPS * STATE
    weight_rows = in_weight.shape[0]
    local_heads = HEADS // group_size
    local_inner = inner // group_size
    starts = segment_offsets(packing, [inner, inner, width_bc, width_bc, HEADS])

    def segment(number, extent):
        return lax.dynamic_slice_in_dim(in_weight, starts[number], extent, 1)

    def per_owner(block):
        return block.reshape(weight_rows, group_size, block.shape[1] // group_size)

    owned = [
        per_owner(segment(0, inner)),
        per_owner(segment(1, inner)),
        per_owner(segment(4, HEADS)),
    ]
    bc_block = jnp.concatenate([segment(2, width_bc), segment(3, width_bc)], axis=1)
    packed = jnp.concatenate(owned, axis=2)
    columns = lax.all_to_all(packed, "tensor", split_axis=1, concat_axis=0, tiled=True).reshape(
        D, packed.shape[2]
    )
    own_width = 2 * local_inner + local_heads
    piece = lax.all_gather(hidden, "tensor", axis=0, tiled=True)
    own_part = jnp.dot(piece, columns, preferred_element_type=jnp.float32)
    row_part = lax.dynamic_slice_in_dim(piece, my_index * weight_rows, weight_rows, 1)
    bc_part = jnp.dot(row_part, bc_block, preferred_element_type=jnp.float32)
    projected = jnp.concatenate([own_part, bc_part], axis=1)
    local_proj = projected[:, :own_width].astype(jnp.bfloat16)
    bc_summed = lax.psum(projected[:, own_width:], "tensor").astype(jnp.bfloat16)
    bc_values = causal_conv(bc_summed, conv_weight[:, inner:])
    gate_raw = local_proj[:, :local_inner]
    x_pre = local_proj[:, local_inner : 2 * local_inner]
    dt_raw = local_proj[:, 2 * local_inner : own_width]
    x_taps = lax.dynamic_slice_in_dim(conv_weight, my_index * local_inner, local_inner, 1)
    x_values = causal_conv(x_pre, x_taps)
    b_full = bc_values[:, :width_bc].astype(jnp.float32).reshape(SEQ, GROUPS, STATE)
    c_full = bc_values[:, width_bc:].astype(jnp.float32).reshape(SEQ, GROUPS, STATE)
    params = lax.dynamic_slice_in_dim(head_params, my_index * local_heads, local_heads, 1)
    local_group = lax.dynamic_slice_in_dim(head_group, my_index * local_heads, local_heads, 0)
    member = (local_group[:, None] == jnp.arange(GROUPS)[None, :]).astype(jnp.float32)
    gated = gated_heads(gate_raw, x_values, b_full, c_full, dt_raw, params, member)
    squares = jnp.sum(gated * gated, axis=2)
    group_part = jnp.dot(squares, member, precision=lax.Precision.HIGHEST)
    group_sq = lax.psum(group_part, "tensor")
    group_ms = group_sq / (HEADS // GROUPS * HEAD_DIM)
    per_head = jnp.dot(group_ms, member.T, precision=lax.Precision.HIGHEST)
    normed = (
        (gated * lax.rsqrt(per_head + epsilon)[:, :, None])
        .reshape(SEQ, local_inner)
        .astype(jnp.bfloat16)
    )
    head_rows = lax.all_to_all(out_weight, "tensor", split_axis=0, concat_axis=1, tiled=True)
    return lax.psum_scatter(
        jnp.dot(normed, head_rows, preferred_element_type=jnp.float32).astype(jnp.bfloat16),
        "tensor",
        scatter_dimension=0,
        tiled=True,
    )


def solution(mesh):
    in_specs = (P(("dp", "tensor"), None), P("tensor", None), P(None, "tensor"), P(), P(), P(), P())
    out_specs = P(("dp", "tensor"), None)
    return jax.shard_map(shards, mesh=mesh, in_specs=in_specs, out_specs=out_specs, check_vma=False)
```

profile of v0, /device:TPU:1, one launch (start us, length us, event | category | flops | bytes accessed | tf_op | source)
XLA Modules:
  0.0 245.0 jit_solution(17126231306000196364)
XLA Ops:
  6.6 0.7 all-gather.2.cloned.1.call-update
  7.3 10.3 %all-to-all-start.1 = ((bf16[16,128,256]{2,1,0:T(8,128)(2,1)}), bf16[16,128,256]{2,1,0:T(8,128)(2,1)S(1)}, u32[]{:S(2)}, u32[]{:S(2)}) async-start(bf16[16,128,256]{2,1,0:T(8,128)(2,1)} %bitcast.87), calls=%async_computation.1 | async-start | bytes 2097152 | tf_op jit(solution)/shard_map/all_to_all | solution.py:115
  17.6 0.6 gather_fusion
  18.5 0.8 fusion.36
  26.2 0.8 constant_dynamic-slice_fusion.3
  29.8 2.4 constant_dynamic-slice_fusion.1
  32.2 2.0 constant_dynamic-slice_fusion.5
  34.2 1.5 pad_maximum_fusion
  35.8 5.8 %all-to-all-start = ((bf16[256,16,260]{0,2,1:T(8,128)(2,1)}), bf16[256,16,260]{0,2,1:T(8,128)(2,1)S(1)}, u32[]{:S(2)}, u32[]{:S(2)}) async-start(bf16[256,16,260]{0,2,1:T(8,128)(2,1)} %pad_maximum_fusion), calls=%async_computation | async-start | bytes 4325376 | tf_op jit(solution)/shard_map/all_to_all | solution.py:82
  41.6 1.3 copy.28
  43.0 23.4 %all-gather.2.cloned.1.call-done = bf16[128,4096]{1,0:T(8,128)(2,1)} async-done(((bf16[8,4096]{1,0:T(8,128)(2,1)}), bf16[128,4096]{1,0:T(8,128)(2,1)}) %all-gather.2.cloned.1.call-update) | async-done | bytes 1048592 | tf_op jit(solution)/shard_map/all_gather | solution.py:86
  66.3 1.7 fusion.5
  68.0 64.2 %all-reduce.3 = bf16[128,2048]{1,0:T(8,128)(2,1)} all-reduce(f32[128,2048]{1,0:T(8,128)S(1)} %fusion.5), channel_id=1, replica_groups=mesh['dp'=32,'tensor'=16] {'tensor'}, use_global_device_ids=true, to_apply=%region_7.8 | all-reduce | flops 262144 | bytes 1572864 | tf_op jit(solution)/shard_map/psum | solution.py:92
  132.3 1.1 convert_element_type.81
  133.4 0.6 multiply_convert_fusion
  134.5 1.0 convolution_bitcast_fusion.1
  135.5 0.4 copy.37
  136.1 1.0 copy.29
  137.3 0.8 fusion.1
  138.6 0.7 fusion
  139.5 0.3 multiply_reduce_fusion
  140.1 31.2 %psum.15 = f32[128,8]{0,1:T(8,128)S(1)} all-reduce(f32[128,8]{0,1:T(8,128)S(1)} %fusion.24), channel_id=1, replica_groups=mesh['dp'=32,'tensor'=16] {'tensor'}, use_global_device_ids=true, to_apply=%region_9.10 | all-reduce | flops 1024 | bytes 8192 | tf_op jit(solution)/shard_map/psum | solution.py:107
  171.6 1.4 convolution_convert_fusion
  173.1 65.1 %reduce-scatter.2.cloned.1.call-done = bf16[8,4096]{1,0:T(8,128)(2,1)} async-done(((bf16[128,4096]{1,0:T(8,128)(2,1)}), bf16[8,4096]{1,0:T(8,128)(2,1)}) %reduce-scatter.2.cloned.1.call-update) | async-done | bytes 65552 | tf_op jit(solution)/shard_map/reduce_scatter | solution.py:116
  (48 shorter events, 2.5 us)
Async XLA Ops:
  6.5 23.1 %copy-start = (f32[3,64]{1,0:T(4,128)S(1)}, f32[3,64]{1,0:T(4,128)}, u32[]{:S(2)}) copy-start(f32[3,64]{1,0:T(4,128)} %param.12) | copy-start | bytes 2308
  6.5 11.1 %copy-start.1 = (s32[5]{0:T(128)S(1)}, s32[5]{0:T(128)}, u32[]{:S(2)}) copy-start(s32[5]{0:T(128)} %constant.64.clone) | copy-start | bytes 64
  6.5 11.1 %copy-start.6 = (s32[5]{0:T(128)S(1)}, s32[5]{0:T(128)}, u32[]{:S(2)}) copy-start(s32[5]{0:T(128)} %param.13) | copy-start | bytes 64
  6.5 23.0 %copy-start.7 = (s32[64]{0:T(128)S(1)}, s32[64]{0:T(128)}, u32[]{:S(2)}) copy-start(s32[64]{0:T(128)} %param.14) | copy-start | bytes 772
  6.5 59.8 %all-gather.2.cloned.1.call-start = ((), (), s32[]{:S(2)}) async-start(), calls=%async_computation.3 | async-start | bytes 1114112 | tf_op jit(solution)/shard_map/all_gather | solution.py:86
  7.3 28.5 %all-to-all-start.1 = ((bf16[16,128,256]{2,1,0:T(8,128)(2,1)}), bf16[16,128,256]{2,1,0:T(8,128)(2,1)S(1)}, u32[]{:S(2)}, u32[]{:S(2)}) async-start(bf16[16,128,256]{2,1,0:T(8,128)(2,1)} %bitcast.87), calls=%async_computation.1 | async-start | bytes 2097152 | tf_op jit(solution)/shard_map/all_to_all | solution.py:115
  34.2 1.5 copy-start.5
  35.8 99.7 %all-to-all-start = ((bf16[256,16,260]{0,2,1:T(8,128)(2,1)}), bf16[256,16,260]{0,2,1:T(8,128)(2,1)S(1)}, u32[]{:S(2)}, u32[]{:S(2)}) async-start(bf16[256,16,260]{0,2,1:T(8,128)(2,1)} %pad_maximum_fusion), calls=%async_computation | async-start | bytes 4325376 | tf_op jit(solution)/shard_map/all_to_all | solution.py:82
  41.6 196.6 %reduce-scatter.2.cloned.1.call-start = ((), (), s32[]{:S(2)}) async-start(), calls=%async_computation.4 | async-start | bytes 1114112 | tf_op jit(solution)/shard_map/reduce_scatter | solution.py:116
  136.1 1.2 copy-start.3
  137.3 1.3 copy-start.4
  137.3 34.3 %copy-start.2 = (bf16[128,16,256]{0,2,1:T(8,128)(2,1)S(1)}, bf16[128,16,256]{0,2,1:T(8,128)(2,1)}, u32[]{:S(2)}) copy-start(bf16[128,16,256]{0,2,1:T(8,128)(2,1)} %copy.28) | copy-start | bytes 3145732
Sparse Core Ops, SparseCore 0:
  9.5 56.7 all-gather.1
  173.2 64.9 reduce-scatter.1
where the time goes:
time: 247 us; the launch traced here: 245 us
  blocking collectives  95.5 us (39%)
  waiting for transfers between devices  89.2 us (36%)
  between operations  23.1 us (9%)
  starting transfers between devices  16.2 us (7%)
  local copies, waits for them, and re-layouts  9.52 us (4%)
  matrix products  6.72 us (3%)
  other arithmetic  4.79 us (2%)
    reduce_scatter x1, waiting for transfers between devices, shards(): lax.psum_scatter(jnp.dot(normed, head_rows, preferred_element_type=jnp.fl...  65.1 us
    psum x1, blocking collectives, shards(): lax.psum(projected[:, own_width:], 'tensor').astype(jnp.bfloat16)  64.2 us
    psum x1, blocking collectives, shards(): group_sq = lax.psum(group_part, 'tensor')  31.2 us
    all_gather x1, waiting for transfers between devices, shards(): piece = lax.all_gather(hidden, 'tensor', axis=0, tiled=True)  23.4 us
    all_to_all x1, starting transfers between devices, shards(): lax.all_to_all(out_weight, 'tensor', split_axis=0, concat_axis=1, tiled=T...  10.3 us
    all_to_all x1, starting transfers between devices, shards(): lax.all_to_all(packed, 'tensor', split_axis=1, concat_axis=0, tiled=True)  5.79 us
    dynamic_slice x3, local copies, waits for them, and re-layouts, segment(): return lax.dynamic_slice_in_dim(in_weight, starts[number], extent, 1)  5.25 us
  transfers between devices with their start and end apart: 4, of which 2 were waited for; matrix products, arithmetic and copies ran while one was open for 6% of the time, Pallas kernels for 0%

commit v1 on v0

v1 whole, which is shorter than its diff:
```python
import functools

import jax
import jax.numpy as jnp
from jax import lax
from jax.experimental import pallas as pl
from jax.experimental.pallas import tpu as pltpu
from jax.sharding import PartitionSpec as P

D = 4096
HEADS = 64
HEAD_DIM = 32
GROUPS = 8
STATE = 128
SEQ = 128
INNER = HEADS * HEAD_DIM
WIDTH_BC = GROUPS * STATE
COLS = 2 * INNER + 2 * WIDTH_BC + HEADS
MEMBERS = 16
CHIPS = MEMBERS // 2
ROWS = D // MEMBERS
HALF = SEQ // 2
PER_GROUP = HEADS // GROUPS
LOCAL = HEADS // MEMBERS
CHANNELS = LOCAL * HEAD_DIM
DT_ROWS = 16
PACKED = 2 * CHANNELS + DT_ROWS

epsilon = 1e-05
F32 = jnp.float32
BF16 = jnp.bfloat16

NT = (((1,), (1,)), ((), ()))


def segment_offsets(packing):
    widths = jnp.where(packing < 2, INNER, jnp.where(packing < 4, WIDTH_BC, HEADS))
    starts = jnp.cumsum(widths) - widths
    numbers = jnp.arange(5)
    return jnp.sum(
        jnp.where(packing[None, :] == numbers[:, None], starts[None, :], 0), axis=1
    ).astype(jnp.int32)


def head_ranks(head_group):
    index = jnp.arange(HEADS)
    before = (head_group[None, :] < head_group[:, None]) | (
        (head_group[None, :] == head_group[:, None]) & (index[None, :] < index[:, None])
    )
    rank = jnp.sum(before.astype(jnp.int32), axis=1)
    order = jnp.sum(
        jnp.where(rank[None, :] == index[:, None], index[None, :], 0), axis=1
    )
    return rank.astype(jnp.int32), order.astype(jnp.int32)


def project_kernel(starts, order, rank, acts, own, peer, out):
    core = lax.axis_index("tensor") % 2
    rows = acts[pl.ds(pl.multiple_of(core * HALF, HALF), HALF), :]
    first, second = rows[:, :ROWS], rows[:, ROWS:]
    is_first = core == 0
    act_own = jnp.where(is_first, first, second)
    act_peer = jnp.where(is_first, second, first)
    act_own = jnp.concatenate([act_own, act_own], axis=0)
    act_peer = jnp.concatenate([act_peer, act_peer], axis=0)

    def multiply(pick):
        return lax.dot_general(
            pick(own), act_own, NT, preferred_element_type=F32
        ) + lax.dot_general(pick(peer), act_peer, NT, preferred_element_type=F32)

    def heads_of(segment, first_head):
        def pick(ref):
            parts = []
            for offset in range(PER_GROUP):
                begin = starts[segment] + order[first_head + offset] * HEAD_DIM
                parts.append(ref[pl.ds(pl.multiple_of(begin, HEAD_DIM), HEAD_DIM), :])
            return jnp.concatenate(parts, axis=0)

        return pick

    def rows_of(segment, begin, extent):
        def pick(ref):
            return ref[pl.ds(pl.multiple_of(starts[segment] + begin, 64), extent), :]

        return pick

    low = lax.broadcasted_iota(jnp.int32, (CHANNELS, SEQ), 1) < HALF

    def chip(index, carry):
        z_part = multiply(heads_of(0, index * PER_GROUP))
        x_part = multiply(heads_of(1, index * PER_GROUP))
        b_part = multiply(rows_of(2, index * STATE, STATE))
        c_part = multiply(rows_of(3, index * STATE, STATE))
        for core_to in range(2):
            picked = slice(core_to * CHANNELS, (core_to + 1) * CHANNELS)
            target = 2 * index + core_to
            out[target, :CHANNELS, :] = jnp.where(low, z_part[picked], b_part).astype(BF16)
            out[target, CHANNELS : 2 * CHANNELS, :] = jnp.where(
                low, x_part[picked], c_part
            ).astype(BF16)
        return carry

    lax.fori_loop(0, CHIPS, chip, 0)

    steps = multiply(rows_of(4, 0, HEADS)).astype(BF16)
    row = lax.broadcasted_iota(jnp.int32, (MEMBERS * DT_ROWS, HEADS), 0)
    inner = row % DT_ROWS
    wanted = jnp.where(inner < LOCAL, (row // DT_ROWS) * LOCAL + inner, -1)
    chosen = (wanted == rank[...]).astype(BF16)
    sorted_steps = jnp.dot(chosen, steps, preferred_element_type=F32).astype(BF16)
    out[:, 2 * CHANNELS :, :] = sorted_steps.reshape(MEMBERS, DT_ROWS, SEQ)


def silu(values):
    return values / (1.0 + jnp.exp(-values))


def mix_kernel(order, params, received, taps_ref, out, taps_scratch):
    member = lax.axis_index("tensor")
    group = member // 2
    heads = [order[member * LOCAL + r] for r in range(LOCAL)]

    halves = []
    for core in range(2):
        total = received[core].astype(F32)
        for chip in range(1, CHIPS):
            total = total + received[2 * chip + core].astype(F32)
        halves.append(total)
    early, late = halves
    lane = lax.broadcasted_iota(jnp.int32, (1, SEQ), 1)
    low = lane < HALF
    main = 2 * CHANNELS
    zx = jnp.where(low, early[:main], pltpu.roll(late[:main], HALF, 1))
    bc = jnp.where(low, pltpu.roll(early[:main], HALF, 1), late[:main])
    steps_raw = jnp.where(low, early[main : main + 8], late[main : main + 8])
    zx = zx.astype(BF16).astype(F32)
    bc = bc.astype(BF16).astype(F32)
    steps_raw = steps_raw.astype(BF16).astype(F32)

    chunks = [
        taps_ref[:, pl.ds(pl.multiple_of((heads[r] // 4) * 128, 128), 128)] for r in range(LOCAL)
    ]
    for base in (INNER, INNER + WIDTH_BC):
        chunks.append(taps_ref[:, pl.ds(pl.multiple_of(base + group * STATE, 128), 128)])
    chunks.append(jnp.zeros((128 - 4 * len(chunks), 128), F32))
    taps_scratch[...] = jnp.concatenate(chunks, axis=0).T

    def conv(values, taps):
        total = taps[:, 3:4] * values
        for tap in range(3):
            shift = 3 - tap
            moved = jnp.where(lane >= shift, pltpu.roll(values, shift, 1), 0.0)
            total = total + taps[:, tap : tap + 1] * moved
        return silu(total).astype(BF16)

    x_taps = jnp.concatenate(
        [
            taps_scratch[pl.ds(pl.multiple_of((heads[r] % 4) * HEAD_DIM, HEAD_DIM), HEAD_DIM), :][
                :, 4 * r : 4 * r + 4
            ]
            for r in range(LOCAL)
        ],
        axis=0,
    )
    x_values = conv(zx[CHANNELS:], x_taps)
    b_values = conv(bc[:CHANNELS], taps_scratch[:, 4 * LOCAL : 4 * LOCAL + 4])
    c_values = conv(bc[CHANNELS:], taps_scratch[:, 4 * LOCAL + 4 : 4 * LOCAL + 8])

    step_rows, rate_rows = [], []
    for r in range(LOCAL):
        raw = steps_raw[r : r + 1] + params[0, heads[r]]
        step = jnp.maximum(raw, 0.0) + jnp.log1p(jnp.exp(-jnp.abs(raw)))
        step_rows.append(step)
        rate_rows.append(-step * jnp.exp(jnp.full((1, SEQ), params[1, heads[r]], F32)))
    running = jnp.concatenate(rate_rows + rate_rows, axis=0)
    for power in range(7):
        shift = 1 << power
        running = running + jnp.where(lane >= shift, pltpu.roll(running, shift, 1), 0.0)
    columns = jnp.concatenate(
        [running[:LOCAL]] + step_rows + [jnp.zeros((128 - 2 * LOCAL, SEQ), F32)], axis=0
    ).T

    scores = lax.dot_general(
        b_values.astype(F32).T.astype(BF16), c_values, (((1,), (0,)), ((), ())),
        preferred_element_type=F32,
    )
    source = lax.broadcasted_iota(jnp.int32, (SEQ, SEQ), 0)
    target = lax.broadcasted_iota(jnp.int32, (SEQ, SEQ), 1)
    causal = source <= target
    gate = silu(zx[:CHANNELS])
    mixed = []
    for r in range(LOCAL):
        spread = running[r : r + 1] - columns[:, r : r + 1]
        decay = jnp.where(causal, jnp.exp(jnp.where(causal, spread, 0.0)), 0.0)
        weights = (decay * scores * columns[:, LOCAL + r : LOCAL + r + 1]).astype(BF16)
        x_head = x_values[r * HEAD_DIM : (r + 1) * HEAD_DIM]
        y_head = jnp.dot(x_head, weights, preferred_element_type=F32)
        mixed.append(y_head + params[2, heads[r]] * x_head.astype(F32))
    gated = jnp.concatenate(mixed, axis=0) * gate
    result = gated.T.astype(BF16)
    for index in range(MEMBERS):
        out[index] = result


def finish_kernel(order, gathered, weight, out):
    total = jnp.zeros((SEQ, ROWS), F32)
    for group in range(GROUPS):
        values = jnp.concatenate([gathered[2 * group], gathered[2 * group + 1]], axis=1)
        wide = values.astype(F32)
        mean_square = jnp.sum(wide * wide, axis=1, keepdims=True) / (PER_GROUP * HEAD_DIM)
        parts = []
        for offset in range(PER_GROUP):
            begin = order[group * PER_GROUP + offset] * HEAD_DIM
            parts.append(weight[pl.ds(pl.multiple_of(begin, HEAD_DIM), HEAD_DIM), :])
        product = jnp.dot(values, jnp.concatenate(parts, axis=0), preferred_element_type=F32)
        total = total + product * lax.rsqrt(mean_square + epsilon)
    out[...] = total.astype(BF16)


SMEM = pl.BlockSpec(memory_space=pltpu.SMEM)
VMEM = pl.BlockSpec(memory_space=pltpu.VMEM)


def shards(hidden, in_weight, out_weight, conv_weight, head_params, packing, head_group):
    starts = segment_offsets(packing)
    rank, order = head_ranks(head_group)

    own = in_weight.T
    peer = lax.ppermute(own, "tensor", [(i, i ^ 1) for i in range(MEMBERS)])
    per_chip = hidden.reshape(8, CHIPS, 2 * ROWS).transpose(1, 0, 2)
    outgoing = jnp.broadcast_to(per_chip[:, None], (CHIPS, 2, 8, 2 * ROWS))
    acts = lax.all_to_all(
        outgoing.reshape(MEMBERS, 8, 2 * ROWS), "tensor", split_axis=0, concat_axis=0, tiled=True
    ).reshape(SEQ, 2 * ROWS)

    partial = pl.pallas_call(
        project_kernel,
        out_shape=jax.ShapeDtypeStruct((MEMBERS, PACKED, SEQ), BF16),
        in_specs=[SMEM, SMEM, VMEM, VMEM, VMEM, VMEM],
        out_specs=VMEM,
        compiler_params=pltpu.CompilerParams(vmem_limit_bytes=20 * 1024 * 1024),
        name="project",
    )(starts, order, rank.reshape(1, HEADS), acts, own, peer)
    received = lax.all_to_all(partial, "tensor", split_axis=0, concat_axis=0, tiled=True)

    gated = pl.pallas_call(
        mix_kernel,
        out_shape=jax.ShapeDtypeStruct((MEMBERS, SEQ, CHANNELS), BF16),
        in_specs=[SMEM, SMEM, VMEM, VMEM],
        out_specs=VMEM,
        scratch_shapes=[pltpu.VMEM((128, 128), F32)],
        compiler_params=pltpu.CompilerParams(vmem_limit_bytes=16 * 1024 * 1024),
        name="mix",
    )(order, head_params, received, conv_weight)
    gathered = lax.all_to_all(gated, "tensor", split_axis=0, concat_axis=0, tiled=True)

    share = pl.pallas_call(
        finish_kernel,
        out_shape=jax.ShapeDtypeStruct((SEQ, ROWS), BF16),
        in_specs=[SMEM, VMEM, VMEM],
        out_specs=VMEM,
        compiler_params=pltpu.CompilerParams(vmem_limit_bytes=16 * 1024 * 1024),
        name="finish",
    )(order, gathered, out_weight)
    pieces = lax.all_to_all(
        share.reshape(MEMBERS, SEQ // MEMBERS, ROWS), "tensor", split_axis=0, concat_axis=0, tiled=True
    )
    return pieces.transpose(1, 0, 2).reshape(SEQ // MEMBERS, D)


def solution(mesh):
    in_specs = (P(("dp", "tensor"), None), P("tensor", None), P(None, "tensor"), P(), P(), P(), P())
    out_specs = P(("dp", "tensor"), None)
    return jax.shard_map(shards, mesh=mesh, in_specs=in_specs, out_specs=out_specs, check_vma=False)
```

time: 247 us -> 72 us (0.29)
  waiting for transfers between devices: 89.2 us -> 2.82 us
  blocking collectives: 95.5 us -> 42.4 us
  between operations: 23.1 us -> 0.06 us
  Pallas kernels: 0 us -> 6.77 us
  matrix products: 6.72 us -> 0 us
  local copies, waits for them, and re-layouts: 9.52 us -> 4.03 us
  starting transfers between devices: 16.2 us -> 12.2 us
    psum x2 -> x0, blocking collectives: 95.5 us -> none  [the longest x1 64.2 us: shards(): lax.psum(projected[:, own_width:], 'tensor').astype(jnp.bfloat16)]
    reduce_scatter x1 -> x0, waiting for transfers between devices: 65.1 us -> none  [shards(): lax.psum_scatter(jnp.dot(normed, head_rows, preferred_element_type=jnp.fl...]
    all_to_all x0 -> x3, blocking collectives: none -> 42.4 us  [the longest x1 20.1 us: shards(): lax.all_to_all(partial, 'tensor', split_axis=0, concat_axis=0, tiled=True)]
    all_gather x1 -> x0, waiting for transfers between devices: 23.4 us -> none  [shards(): piece = lax.all_gather(hidden, 'tensor', axis=0, tiled=True)]
    all_to_all x2 -> x1, starting transfers between devices: 16.1 us -> 3.41 us  [shards(): lax.all_to_all(outgoing.reshape(MEMBERS, 8, 2 * ROWS), 'tensor', split_ax...]
    ppermute x0 -> x1, starting transfers between devices: none -> 8.78 us  [shards(): peer = lax.ppermute(own, 'tensor', [(i, i ^ 1) for i in range(MEMBERS)])]
    pallas_call x0 -> x3, Pallas kernels: none -> 6.77 us  [the longest x1 3.87 us: shards(): pl.pallas_call(project_kernel, out_shape=jax.ShapeDtypeStruct((MEMBERS, P...]
    dot_general x9 -> x0, matrix products: 6.72 us -> none  [the longest x1 1.71 us: shards(): bc_part = jnp.dot(row_part, bc_block, preferred_element_type=jnp.float32)]
  transfers between devices with their start and end apart: 4 -> 2, of which waited for: 2 -> 1; matrix products, arithmetic and copies ran while one was open for 6% -> 7% of each run, Pallas kernels for 0% -> 0%
where the time goes in v1:
time: 72 us; the launch traced here: 71.5 us
  blocking collectives  42.4 us (59%)
  starting transfers between devices  12.2 us (17%)
  Pallas kernels  6.77 us (9%)
  local copies, waits for them, and re-layouts  4.03 us (6%)
  other arithmetic  3.29 us (5%)
  waiting for transfers between devices  2.82 us (4%)
    all_to_all x1, blocking collectives, shards(): lax.all_to_all(partial, 'tensor', split_axis=0, concat_axis=0, tiled=True)  20.1 us
    all_to_all x1, blocking collectives, shards(): lax.all_to_all(gated, 'tensor', split_axis=0, concat_axis=0, tiled=True)  12.8 us
    all_to_all x1, blocking collectives, shards(): lax.all_to_all(share.reshape(MEMBERS, SEQ // MEMBERS, ROWS), 'tensor', sp...  9.45 us
    ppermute x1, starting transfers between devices, shards(): peer = lax.ppermute(own, 'tensor', [(i, i ^ 1) for i in range(MEMBERS)])  8.78 us
    pallas_call x1, Pallas kernels, shards(): pl.pallas_call(project_kernel, out_shape=jax.ShapeDtypeStruct((MEMBERS, P...  3.87 us
    all_to_all x1, starting transfers between devices, shards(): lax.all_to_all(outgoing.reshape(MEMBERS, 8, 2 * ROWS), 'tensor', split_ax...  3.41 us
    all_to_all x1, waiting for transfers between devices, shards(): lax.all_to_all(outgoing.reshape(MEMBERS, 8, 2 * ROWS), 'tensor', split_ax...  2.82 us
    unnamed x9, local copies, waits for them, and re-layouts  2.54 us
  transfers between devices with their start and end apart: 2, of which 1 were waited for; matrix products, arithmetic and copies ran while one was open for 7% of the time, Pallas kernels for 0%

profile of v1, /device:TPU:1, one launch (start us, length us, event | category | flops | bytes accessed | tf_op | source)
XLA Modules:
  0.0 71.5 jit_solution(17434593739268742605)
XLA Ops:
  0.0 8.8 %collective-permute-start = (bf16[6208,256]{1,0:T(8,128)(2,1)}, bf16[6208,256]{1,0:T(8,128)(2,1)S(1)}, u32[]{:S(2)}, u32[]{:S(2)}) collective-permute-start(bf16[6208,256]{1,0:T(8,128)(2,1)} %bitcast.15), channel_id=1, source_target_pairs={{0,1},{1,0},{2,3},{3,2},{4,5},{5,4},{6,7},{7,6},{8,9},{9,8},{10,11... | collective-permute-start | bytes 9535496 | tf_op jit(solution)/shard_map/ppermute | solution.py:230
  8.8 1.5 %broadcast_in_dim.61 = bf16[8,2,8,512]{3,2,1,0:T(8,128)(2,1)} broadcast(bf16[8,8,512]{2,1,0:T(8,128)(2,1)} %bitcast.21), dimensions={0,2,3} | broadcast | bytes 196608 | tf_op jit(solution)/shard_map/broadcast_in_dim | solution.py:232
  10.3 3.4 %all-to-all-start = ((bf16[16,8,512]{2,1,0:T(8,128)(2,1)}), bf16[16,8,512]{2,1,0:T(8,128)(2,1)S(1)}, u32[]{:S(2)}, u32[]{:S(2)}) async-start(bf16[16,8,512]{2,1,0:T(8,128)(2,1)} %bitcast.5), calls=%async_computation | async-start | bytes 262144 | tf_op jit(solution)/shard_map/all_to_all | solution.py:233
  13.7 0.7 fusion.2
  14.3 0.2 reduce-window.9
  14.5 0.9 %convert_reduce_fusion = s32[64]{0:T(128)S(1)} fusion(s32[64]{0:T(128)} %param.13), kind=kLoop, calls=%fused_computation.2 | loop fusion | flops 28608 | bytes 512 | tf_op jit(solution)/shard_map/reduce_sum | solution.py:50
  15.4 0.7 bitcast_subtract_fusion
  16.1 0.8 %select_reduce_fusion.1.starts = s32[5]{0:T(128)S(1)} fusion(s32[5]{0:T(128)S(1)} %bitcast_subtract_fusion, s32[5]{0:T(128)} %param.12), kind=kLoop, calls=%fused_computation.6 | loop fusion | flops 70 | bytes 60 | tf_op jit(solution)/shard_map/reduce_sum | solution.py:40
  16.9 0.1 select_reduce_fusion.order
  17.0 2.8 %all-to-all-done = bf16[16,8,512]{2,1,0:T(8,128)(2,1)S(1)} async-done(((bf16[16,8,512]{2,1,0:T(8,128)(2,1)}), bf16[16,8,512]{2,1,0:T(8,128)(2,1)S(1)}, u32[]{:S(2)}, u32[]{:S(2)}) %all-to-all-start) | async-done | bytes 131104 | tf_op jit(solution)/shard_map/all_to_all | solution.py:233
  19.8 0.0 collective-permute-done.peer
  19.8 0.0 copy-start
  19.8 1.9 %copy-done = bf16[256,6208]{0,1:T(8,128)(2,1)S(1)} copy-done((bf16[256,6208]{0,1:T(8,128)(2,1)S(1)}, bf16[256,6208]{0,1:T(8,128)(2,1)}, u32[]{:S(2)}) %copy-start) | copy-done | bytes 3178520
  21.7 3.9 %project.1 = bf16[16,272,128]{2,1,0:T(8,128)(2,1)S(1)} custom-call(s32[5]{0:T(128)S(1)} %select_reduce_fusion.1.starts, s32[64]{0:T(128)S(1)} %select_reduce_fusion.order, s32[1,64]{1,0:T(1,128)S(1)} %bitcast.19, bf16[128,512]{1,0:T(8,128)(2,1)S(1)} %bitcast.17, bf16[6208,256]{1,0:T(8,128)(2,1)S(1)} %bitcast.16, bf16[6208,256]{1,0:T(8,128)(2,1)S(1)} %collective-permute-done.peer), custom_call_target="tpu_custom_call" | custom-call | tf_op jit(solution)/shard_map/project/pallas_call | solution.py:237
  25.6 0.0 copy-start.1
  25.6 20.1 %all_to_all.20.received = bf16[16,272,128]{2,1,0:T(8,128)(2,1)S(1)} all-to-all(bf16[16,272,128]{2,1,0:T(8,128)(2,1)S(1)} %project.1), channel_id=1, replica_groups=mesh['dp'=32,'tensor'=16] {'tensor'}, dimensions={0} | all-to-all | bytes 2228224 | tf_op jit(solution)/shard_map/all_to_all | solution.py:245
  45.8 0.0 copy-done.2
  45.8 0.0 copy-done.3
  45.8 2.0 %mix.1 = bf16[16,128,128]{2,1,0:T(8,128)(2,1)S(1)} custom-call(s32[64]{0:T(128)S(1)} %select_reduce_fusion.order, f32[3,64]{1,0:T(4,128)S(1)} %copy-done.3, bf16[16,272,128]{2,1,0:T(8,128)(2,1)S(1)} %all_to_all.20.received, f32[4,4096]{1,0:T(4,128)S(1)} %copy-done.2), custom_call_target="tpu_custom_call" | custom-call | tf_op jit(solution)/shard_map/mix/pallas_call | solution.py:247
  47.8 12.8 %all_to_all.21.gathered = bf16[16,128,128]{2,1,0:T(8,128)(2,1)S(1)} all-to-all(bf16[16,128,128]{2,1,0:T(8,128)(2,1)S(1)} %mix.1), channel_id=1, replica_groups=mesh['dp'=32,'tensor'=16] {'tensor'}, dimensions={0} | all-to-all | bytes 1048576 | tf_op jit(solution)/shard_map/all_to_all | solution.py:256
  60.6 0.0 copy-done.1
  60.6 0.9 %finish.1 = bf16[128,256]{1,0:T(8,128)(2,1)S(1)} custom-call(s32[64]{0:T(128)S(1)} %select_reduce_fusion.order, bf16[16,128,128]{2,1,0:T(8,128)(2,1)S(1)} %all_to_all.21.gathered, bf16[2048,256]{1,0:T(8,128)(2,1)S(1)} %copy-done.1), custom_call_target="tpu_custom_call" | custom-call | tf_op jit(solution)/shard_map/finish/pallas_call | solution.py:258
  61.4 9.5 %all_to_all.22 = bf16[16,8,256]{2,1,0:T(8,128)(2,1)S(1)} all-to-all(bf16[16,8,256]{2,1,0:T(8,128)(2,1)S(1)} %bitcast.18), channel_id=1, replica_groups=mesh['dp'=32,'tensor'=16] {'tensor'}, dimensions={0} | all-to-all | bytes 131072 | tf_op jit(solution)/shard_map/all_to_all | solution.py:266
  70.9 0.6 copy.9
  (2 shorter events, 0.0 us)
Async XLA Ops:
  0.0 19.8 %collective-permute-start = (bf16[6208,256]{1,0:T(8,128)(2,1)}, bf16[6208,256]{1,0:T(8,128)(2,1)S(1)}, u32[]{:S(2)}, u32[]{:S(2)}) collective-permute-start(bf16[6208,256]{1,0:T(8,128)(2,1)} %bitcast.15), channel_id=1, source_target_pairs={{0,1},{1,0},{2,3},{3,2},{4,5},{5,4},{6,7},{7,6},{8,9},{9,8},{10,11... | collective-permute-start | bytes 9535496 | tf_op jit(solution)/shard_map/ppermute | solution.py:230
  10.3 9.5 %all-to-all-start = ((bf16[16,8,512]{2,1,0:T(8,128)(2,1)}), bf16[16,8,512]{2,1,0:T(8,128)(2,1)S(1)}, u32[]{:S(2)}, u32[]{:S(2)}) async-start(bf16[16,8,512]{2,1,0:T(8,128)(2,1)} %bitcast.5), calls=%async_computation | async-start | bytes 262144 | tf_op jit(solution)/shard_map/all_to_all | solution.py:233
  19.8 1.9 %copy-start = (bf16[256,6208]{0,1:T(8,128)(2,1)S(1)}, bf16[256,6208]{0,1:T(8,128)(2,1)}, u32[]{:S(2)}) copy-start(bf16[256,6208]{0,1:T(8,128)(2,1)} %param.8) | copy-start | bytes 9535492
  21.7 24.0 %copy-start.2 = (f32[4,4096]{1,0:T(4,128)S(1)}, f32[4,4096]{1,0:T(4,128)}, u32[]{:S(2)}) copy-start(f32[4,4096]{1,0:T(4,128)} %taps_ref.1) | copy-start | bytes 196612
  21.7 24.0 %copy-start.3 = (f32[3,64]{1,0:T(4,128)S(1)}, f32[3,64]{1,0:T(4,128)}, u32[]{:S(2)}) copy-start(f32[3,64]{1,0:T(4,128)} %params.1) | copy-start | bytes 2308
  25.6 35.0 %copy-start.1 = (bf16[2048,256]{1,0:T(8,128)(2,1)S(1)}, bf16[2048,256]{1,0:T(8,128)(2,1)}, u32[]{:S(2)}) copy-start(bf16[2048,256]{1,0:T(8,128)(2,1)} %weight.1) | copy-start | bytes 3145732

commit v2 on v1

v2 whole, which is shorter than its diff:
```python
import functools

import jax
import jax.numpy as jnp
from jax import lax
from jax.experimental import pallas as pl
from jax.experimental.pallas import tpu as pltpu
from jax.sharding import PartitionSpec as P

D = 4096
HEADS = 64
HEAD_DIM = 32
GROUPS = 8
STATE = 128
SEQ = 128
INNER = HEADS * HEAD_DIM
WIDTH_BC = GROUPS * STATE
COLS = 2 * INNER + 2 * WIDTH_BC + HEADS
MEMBERS = 16
CHIPS = MEMBERS // 2
ROWS = D // MEMBERS
HALF = SEQ // 2
PER_GROUP = HEADS // GROUPS
LOCAL = HEADS // MEMBERS
CHANNELS = LOCAL * HEAD_DIM
DT_ROWS = 16
PACKED = 2 * CHANNELS + DT_ROWS

epsilon = 1e-05
F32 = jnp.float32
BF16 = jnp.bfloat16

NT = (((1,), (1,)), ((), ()))


CHIP_GROUPS = [[2 * chip + core for chip in range(CHIPS)] for core in range(2)]
ORDER, STARTS = 0, HEADS


def stage_kernel(packing, head_group, plan, arrange, filled):
    begin = jnp.int32(0)
    for place in range(5):
        number = packing[place]
        plan[STARTS + number] = begin
        begin = begin + jnp.where(number < 2, INNER, jnp.where(number < 4, WIDTH_BC, HEADS))
    for spare in range(STARTS + 5, 80):
        plan[spare] = 0
    for group in range(GROUPS):
        filled[group] = 0

    def place_head(head, carry):
        group = head_group[head]
        position = filled[group]
        plan[ORDER + group * PER_GROUP + position] = head
        filled[group] = position + 1
        return carry

    lax.fori_loop(0, HEADS, place_head, 0, unroll=8)

    source = lax.broadcasted_iota(jnp.int32, (2 * SEQ, 2 * SEQ), 0)
    target = lax.broadcasted_iota(jnp.int32, (2 * SEQ, 2 * SEQ), 1)
    column = source % HALF
    token = 16 * (column // 8) + 8 * (source // SEQ) + column % 8
    wanted = token + SEQ * ((source // HALF) % 2)
    arrange[...] = jnp.where(wanted == target, 1.0, 0.0).astype(BF16)


def project_kernel(plan, acts, own, peer, out, steps_ref, sorted_ref):
    core = lax.axis_index("tensor") % 2
    rows = acts[...]
    first, second = rows[:, :ROWS], rows[:, ROWS:]
    is_first = core == 0
    both = jnp.concatenate(
        [jnp.where(is_first, first, second), jnp.where(is_first, second, first)], axis=1
    )
    both = jnp.concatenate([both, both], axis=0)

    def multiply(begins, extent):
        picked = []
        for begin in begins:
            where = pl.ds(pl.multiple_of(begin, HEAD_DIM), extent)
            picked.append(jnp.concatenate([own[where, :], peer[where, :]], axis=1))
        return lax.dot_general(
            jnp.concatenate(picked, axis=0), both, NT, preferred_element_type=F32
        )

    steps_ref[...] = multiply([plan[STARTS + 4]], HEADS)
    sorted_ref[...] = jnp.zeros_like(sorted_ref)
    for member in range(MEMBERS):
        for r in range(LOCAL):
            sorted_ref[pl.ds(member * DT_ROWS + r, 1), :] = steps_ref[
                pl.ds(plan[ORDER + member * LOCAL + r], 1), :
            ]
    out[:, 2 * CHANNELS :, :] = sorted_ref[...].astype(BF16).reshape(MEMBERS, DT_ROWS, SEQ)

    low = lax.broadcasted_iota(jnp.int32, (CHANNELS, SEQ), 1) < HALF

    def chip(index, carry):
        heads = [plan[ORDER + index * PER_GROUP + offset] for offset in range(PER_GROUP)]
        z_part = multiply([plan[STARTS] + head * HEAD_DIM for head in heads], HEAD_DIM)
        x_part = multiply([plan[STARTS + 1] + head * HEAD_DIM for head in heads], HEAD_DIM)
        bc_part = multiply([plan[STARTS + 2] + index * STATE, plan[STARTS + 3] + index * STATE], STATE)
        for core_to in range(2):
            picked = slice(core_to * CHANNELS, (core_to + 1) * CHANNELS)
            target = 2 * index + core_to
            out[target, :CHANNELS, :] = jnp.where(
                low, z_part[picked], bc_part[:STATE]
            ).astype(BF16)
            out[target, CHANNELS : 2 * CHANNELS, :] = jnp.where(
                low, x_part[picked], bc_part[STATE:]
            ).astype(BF16)
        return carry

    lax.fori_loop(0, CHIPS, chip, 0, unroll=2)


def silu(values):
    return values / (1.0 + jnp.exp(-values))


def mix_kernel(plan, params, received, taps_ref, arrange, out, taps_scratch):
    member = lax.axis_index("tensor")
    group = member // 2
    heads = [plan[ORDER + member * LOCAL + r] for r in range(LOCAL)]

    halves = []
    for core in range(2):
        total = received[core].astype(F32)
        for chip in range(1, CHIPS):
            total = total + received[2 * chip + core].astype(F32)
        halves.append(total)
    lane = lax.broadcasted_iota(jnp.int32, (1, SEQ), 1)
    summed = jnp.concatenate([half.astype(BF16) for half in halves], axis=1)
    ordered = jnp.dot(summed, arrange[...], preferred_element_type=F32)
    zx = ordered[: 2 * CHANNELS, :SEQ]
    bc = ordered[: 2 * CHANNELS, SEQ:]
    steps_raw = ordered[2 * CHANNELS :, :SEQ]

    chunks = [
        taps_ref[:, pl.ds(pl.multiple_of((heads[r] // 4) * 128, 128), 128)] for r in range(LOCAL)
    ]
    for base in (INNER, INNER + WIDTH_BC):
        chunks.append(taps_ref[:, pl.ds(pl.multiple_of(base + group * STATE, 128), 128)])
    chunks.append(jnp.zeros((128 - 4 * len(chunks), 128), F32))
    taps_scratch[...] = jnp.concatenate(chunks, axis=0).T

    def conv(values, taps):
        total = taps[:, 3:4] * values
        for tap in range(3):
            shift = 3 - tap
            moved = jnp.where(lane >= shift, pltpu.roll(values, shift, 1), 0.0)
            total = total + taps[:, tap : tap + 1] * moved
        return silu(total).astype(BF16)

    x_taps = jnp.concatenate(
        [
            taps_scratch[pl.ds(pl.multiple_of((heads[r] % 4) * HEAD_DIM, HEAD_DIM), HEAD_DIM), :][
                :, 4 * r : 4 * r + 4
            ]
            for r in range(LOCAL)
        ],
        axis=0,
    )
    x_values = conv(zx[CHANNELS:], x_taps)
    b_values = conv(bc[:CHANNELS], taps_scratch[:, 4 * LOCAL : 4 * LOCAL + 4])
    c_values = conv(bc[CHANNELS:], taps_scratch[:, 4 * LOCAL + 4 : 4 * LOCAL + 8])

    step_rows, rate_rows = [], []
    for r in range(LOCAL):
        raw = steps_raw[r : r + 1] + params[0, heads[r]]
        step = jnp.maximum(raw, 0.0) + jnp.log1p(jnp.exp(-jnp.abs(raw)))
        step_rows.append(step)
        rate_rows.append(-step * jnp.exp(jnp.full((1, SEQ), params[1, heads[r]], F32)))
    running = jnp.concatenate(rate_rows + rate_rows, axis=0)
    for power in range(7):
        shift = 1 << power
        running = running + jnp.where(lane >= shift, pltpu.roll(running, shift, 1), 0.0)
    columns = jnp.concatenate(
        [running[:LOCAL]] + step_rows + [jnp.zeros((128 - 2 * LOCAL, SEQ), F32)], axis=0
    ).T

    scores = lax.dot_general(
        b_values.astype(F32).T.astype(BF16), c_values, (((1,), (0,)), ((), ())),
        preferred_element_type=F32,
    )
    source = lax.broadcasted_iota(jnp.int32, (SEQ, SEQ), 0)
    target = lax.broadcasted_iota(jnp.int32, (SEQ, SEQ), 1)
    causal = source <= target
    gate = silu(zx[:CHANNELS])
    mixed = []
    for r in range(LOCAL):
        spread = running[r : r + 1] - columns[:, r : r + 1]
        decay = jnp.where(causal, jnp.exp(jnp.where(causal, spread, 0.0)), 0.0)
        weights = (decay * scores * columns[:, LOCAL + r : LOCAL + r + 1]).astype(BF16)
        x_head = x_values[r * HEAD_DIM : (r + 1) * HEAD_DIM]
        y_head = jnp.dot(x_head, weights, preferred_element_type=F32)
        mixed.append(y_head + params[2, heads[r]] * x_head.astype(F32))
    gated = jnp.concatenate(mixed, axis=0) * gate
    result = gated.T.astype(BF16)
    for index in range(MEMBERS):
        out[index] = result


def finish_kernel(plan, gathered, weight, out):
    total = jnp.zeros((SEQ, ROWS), F32)
    for group in range(GROUPS):
        values = jnp.concatenate([gathered[2 * group], gathered[2 * group + 1]], axis=1)
        wide = values.astype(F32)
        mean_square = jnp.sum(wide * wide, axis=1, keepdims=True) / (PER_GROUP * HEAD_DIM)
        parts = []
        for offset in range(PER_GROUP):
            begin = plan[ORDER + group * PER_GROUP + offset] * HEAD_DIM
            parts.append(weight[pl.ds(pl.multiple_of(begin, HEAD_DIM), HEAD_DIM), :])
        product = jnp.dot(values, jnp.concatenate(parts, axis=0), preferred_element_type=F32)
        total = total + product * lax.rsqrt(mean_square + epsilon)
    out[...] = total.astype(BF16)


SMEM = pl.BlockSpec(memory_space=pltpu.SMEM)
VMEM = pl.BlockSpec(memory_space=pltpu.VMEM)


def shards(hidden, in_weight, out_weight, conv_weight, head_params, packing, head_group):
    own = in_weight.T
    peer = lax.ppermute(own, "tensor", [(i, i ^ 1) for i in range(MEMBERS)])
    per_chip = hidden.reshape(SEQ // MEMBERS, CHIPS, 2 * ROWS).transpose(1, 0, 2)
    acts = lax.all_to_all(
        per_chip, "tensor", split_axis=0, concat_axis=0, tiled=True, axis_index_groups=CHIP_GROUPS
    ).reshape(HALF, 2 * ROWS)

    plan, arrange = pl.pallas_call(
        stage_kernel,
        out_shape=(
            jax.ShapeDtypeStruct((80,), jnp.int32),
            jax.ShapeDtypeStruct((2 * SEQ, 2 * SEQ), BF16),
        ),
        in_specs=[SMEM, SMEM],
        out_specs=(SMEM, VMEM),
        scratch_shapes=[pltpu.SMEM((GROUPS,), jnp.int32)],
        compiler_params=pltpu.CompilerParams(vmem_limit_bytes=2 * 1024 * 1024),
        cost_estimate=pl.CostEstimate(flops=4 * 10**9, bytes_accessed=4 * 10**6, transcendentals=0),
        name="stage",
    )(packing, head_group)

    partial = pl.pallas_call(
        project_kernel,
        out_shape=jax.ShapeDtypeStruct((MEMBERS, PACKED, SEQ), BF16),
        in_specs=[SMEM, VMEM, VMEM, VMEM],
        out_specs=VMEM,
        scratch_shapes=[pltpu.VMEM((HEADS, SEQ), F32), pltpu.VMEM((MEMBERS * DT_ROWS, SEQ), F32)],
        compiler_params=pltpu.CompilerParams(vmem_limit_bytes=16 * 1024 * 1024),
        name="project",
    )(plan, acts, own, peer)
    received = lax.all_to_all(partial, "tensor", split_axis=0, concat_axis=0, tiled=True)

    gated = pl.pallas_call(
        mix_kernel,
        out_shape=jax.ShapeDtypeStruct((MEMBERS, SEQ, CHANNELS), BF16),
        in_specs=[SMEM, SMEM, VMEM, VMEM, VMEM],
        out_specs=VMEM,
        scratch_shapes=[pltpu.VMEM((128, 128), F32)],
        compiler_params=pltpu.CompilerParams(vmem_limit_bytes=8 * 1024 * 1024),
        name="mix",
    )(plan, head_params, received, conv_weight, arrange)
    gathered = lax.all_to_all(gated, "tensor", split_axis=0, concat_axis=0, tiled=True)

    share = pl.pallas_call(
        finish_kernel,
        out_shape=jax.ShapeDtypeStruct((SEQ, ROWS), BF16),
        in_specs=[SMEM, VMEM, VMEM],
        out_specs=VMEM,
        compiler_params=pltpu.CompilerParams(vmem_limit_bytes=8 * 1024 * 1024),
        name="finish",
    )(plan, gathered, out_weight)
    pieces = lax.all_to_all(
        share.reshape(MEMBERS, SEQ // MEMBERS, ROWS), "tensor", split_axis=0, concat_axis=0, tiled=True
    )
    return pieces.transpose(1, 0, 2).reshape(SEQ // MEMBERS, D)


def solution(mesh):
    in_specs = (P(("dp", "tensor"), None), P("tensor", None), P(None, "tensor"), P(), P(), P(), P())
    out_specs = P(("dp", "tensor"), None)
    return jax.shard_map(shards, mesh=mesh, in_specs=in_specs, out_specs=out_specs, check_vma=False)
```

time: 72 us -> 68.5 us (0.951)
  other arithmetic: 3.29 us -> 0 us
  local copies, waits for them, and re-layouts: 4.03 us -> 1.95 us
  Pallas kernels: 6.77 us -> 8.81 us
    reduce_sum x3 -> x0, other arithmetic: 1.78 us -> none  [the longest x1 0.91 us: head_ranks(): rank = jnp.sum(before.astype(jnp.int32), axis=1)]
    broadcast_in_dim x1 -> x0, local copies, waits for them, and re-layouts: 1.49 us -> none  [shards(): outgoing = jnp.broadcast_to(per_chip[:, None], (CHIPS, 2, 8, 2 * ROWS))]
    pallas_call x0 -> x1, Pallas kernels: none -> 1.48 us  [shards(): pl.pallas_call(stage_kernel, out_shape=(jax.ShapeDtypeStruct((80,), jnp.i...]
    another operation x2 -> x0, other arithmetic: 0.84 us -> none
    unnamed x9 -> x13, local copies, waits for them, and re-layouts: 2.54 us -> 1.95 us
  transfers between devices with their start and end apart: 2 -> 2, of which waited for: 1 -> 1; matrix products, arithmetic and copies ran while one was open for 7% -> 0% of each run, Pallas kernels for 0% -> 2%
where the time goes in v2:
time: 68.5 us; the launch traced here: 68.1 us
  blocking collectives  42.8 us (62%)
  starting transfers between devices  12.1 us (18%)
  Pallas kernels  8.81 us (13%)
  waiting for transfers between devices  2.32 us (3%)
  local copies, waits for them, and re-layouts  1.95 us (3%)
    all_to_all x1, blocking collectives, shards(): lax.all_to_all(partial, 'tensor', split_axis=0, concat_axis=0, tiled=True)  20.6 us
    all_to_all x1, blocking collectives, shards(): lax.all_to_all(gated, 'tensor', split_axis=0, concat_axis=0, tiled=True)  12.8 us
    all_to_all x1, blocking collectives, shards(): lax.all_to_all(share.reshape(MEMBERS, SEQ // MEMBERS, ROWS), 'tensor', sp...  9.45 us
    ppermute x1, starting transfers between devices, shards(): peer = lax.ppermute(own, 'tensor', [(i, i ^ 1) for i in range(MEMBERS)])  8.78 us
    pallas_call x1, Pallas kernels, shards(): pl.pallas_call(project_kernel, out_shape=jax.ShapeDtypeStruct((MEMBERS, P...  4.45 us
    all_to_all x1, starting transfers between devices, shards(): lax.all_to_all(per_chip, 'tensor', split_axis=0, concat_axis=0, tiled=Tru...  3.36 us
    all_to_all x1, waiting for transfers between devices, shards(): lax.all_to_all(per_chip, 'tensor', split_axis=0, concat_axis=0, tiled=Tru...  2.31 us
    pallas_call x1, Pallas kernels, shards(): pl.pallas_call(mix_kernel, out_shape=jax.ShapeDtypeStruct((MEMBERS, SEQ,...  2.02 us
  transfers between devices with their start and end apart: 2, of which 1 were waited for; matrix products, arithmetic and copies ran while one was open for 0% of the time, Pallas kernels for 2%

profile of v2, /device:TPU:1, one launch (start us, length us, event | category | flops | bytes accessed | tf_op | source)
XLA Modules:
  0.0 68.1 jit_solution(17702654812261230313)
XLA Ops:
  0.0 8.8 %collective-permute-start = (bf16[6208,256]{1,0:T(8,128)(2,1)}, bf16[6208,256]{1,0:T(8,128)(2,1)}, u32[]{:S(2)}, u32[]{:S(2)}) collective-permute-start(bf16[6208,256]{1,0:T(8,128)(2,1)} %bitcast.9), channel_id=1, source_target_pairs={{0,1},{1,0},{2,3},{3,2},{4,5},{5,4},{6,7},{7,6},{8,9},{9,8},{10,11... | collective-permute-start | bytes 9535496 | tf_op jit(solution)/shard_map/ppermute | solution.py:225
  8.8 3.4 %all-to-all-start = ((bf16[8,8,512]{2,1,0:T(8,128)(2,1)}), bf16[8,8,512]{2,1,0:T(8,128)(2,1)S(1)}, u32[]{:S(2)}, u32[]{:S(2)}) async-start(bf16[8,8,512]{2,1,0:T(8,128)(2,1)} %bitcast.14), calls=%async_computation | async-start | bytes 131072 | tf_op jit(solution)/shard_map/all_to_all | solution.py:227
  12.2 0.0 copy-start.4
  12.2 0.6 copy-done.4
  12.8 0.0 copy-start.5
  12.8 0.7 copy-done.5
  13.5 0.0 copy-start
  13.5 1.5 %stage.1 = (s32[80]{0:T(128)S(1)}, bf16[256,256]{1,0:T(8,128)(2,1)S(1)}) custom-call(s32[5]{0:T(128)S(1)} %copy-done.4, s32[64]{0:T(128)S(1)} %copy-done.5), custom_call_target="tpu_custom_call" | custom-call | flops 4000000000 | bytes 4000000 | tf_op jit(solution)/shard_map/stage/pallas_call | solution.py:231
  15.0 2.3 %all-to-all-done = bf16[8,8,512]{2,1,0:T(8,128)(2,1)S(1)} async-done(((bf16[8,8,512]{2,1,0:T(8,128)(2,1)}), bf16[8,8,512]{2,1,0:T(8,128)(2,1)S(1)}, u32[]{:S(2)}, u32[]{:S(2)}) %all-to-all-start) | async-done | bytes 65568 | tf_op jit(solution)/shard_map/all_to_all | solution.py:227
  17.3 0.0 collective-permute-done.peer
  17.3 0.0 copy-done
  17.3 0.0 copy-start.2
  17.3 0.0 copy-start.3
  17.3 4.4 %project.1 = bf16[16,272,128]{2,1,0:T(8,128)(2,1)S(1)} custom-call(s32[80]{0:T(128)S(1)} %get-tuple-element.7.plan, bf16[64,512]{1,0:T(8,128)(2,1)S(1)} %bitcast.11, bf16[6208,256]{1,0:T(8,128)(2,1)S(1)} %bitcast.10, bf16[6208,256]{1,0:T(8,128)(2,1)} %collective-permute-done.peer), custom_call_target="tpu_custom_call" | custom-call | tf_op jit(solution)/shard_map/project/pallas_call | solution.py:245
  21.8 0.0 copy-start.1
  21.8 20.6 %all_to_all.20.received = bf16[16,272,128]{2,1,0:T(8,128)(2,1)S(1)} all-to-all(bf16[16,272,128]{2,1,0:T(8,128)(2,1)S(1)} %project.1), channel_id=1, replica_groups=mesh['dp'=32,'tensor'=16] {'tensor'}, dimensions={0} | all-to-all | bytes 2228224 | tf_op jit(solution)/shard_map/all_to_all | solution.py:254
  42.4 0.0 copy-done.2
  42.4 0.0 copy-done.3
  42.4 2.0 %mix.1 = bf16[16,128,128]{2,1,0:T(8,128)(2,1)S(1)} custom-call(s32[80]{0:T(128)S(1)} %get-tuple-element.7.plan, f32[3,64]{1,0:T(4,128)S(1)} %copy-done.3, bf16[16,272,128]{2,1,0:T(8,128)(2,1)S(1)} %all_to_all.20.received, f32[4,4096]{1,0:T(4,128)S(1)} %copy-done.2, bf16[256,256]{1,0:T(8,128)(2,1)S(1)} %get-tuple-element.8.arrange), custom_call_target="tpu_custom_call" | custom-call | tf_op jit(solution)/shard_map/mix/pallas_call | solution.py:256
  44.4 12.8 %all_to_all.21.gathered = bf16[16,128,128]{2,1,0:T(8,128)(2,1)S(1)} all-to-all(bf16[16,128,128]{2,1,0:T(8,128)(2,1)S(1)} %mix.1), channel_id=1, replica_groups=mesh['dp'=32,'tensor'=16] {'tensor'}, dimensions={0} | all-to-all | bytes 1048576 | tf_op jit(solution)/shard_map/all_to_all | solution.py:265
  57.2 0.0 copy-done.1
  57.2 0.9 %finish.1 = bf16[128,256]{1,0:T(8,128)(2,1)S(1)} custom-call(s32[80]{0:T(128)S(1)} %get-tuple-element.7.plan, bf16[16,128,128]{2,1,0:T(8,128)(2,1)S(1)} %all_to_all.21.gathered, bf16[2048,256]{1,0:T(8,128)(2,1)S(1)} %copy-done.1), custom_call_target="tpu_custom_call" | custom-call | tf_op jit(solution)/shard_map/finish/pallas_call | solution.py:267
  58.1 9.4 %all_to_all.22 = bf16[16,8,256]{2,1,0:T(8,128)(2,1)S(1)} all-to-all(bf16[16,8,256]{2,1,0:T(8,128)(2,1)S(1)} %bitcast.12), channel_id=1, replica_groups=mesh['dp'=32,'tensor'=16] {'tensor'}, dimensions={0} | all-to-all | bytes 131072 | tf_op jit(solution)/shard_map/all_to_all | solution.py:275
  67.5 0.6 copy.9
Async XLA Ops:
  0.0 17.3 %collective-permute-start = (bf16[6208,256]{1,0:T(8,128)(2,1)}, bf16[6208,256]{1,0:T(8,128)(2,1)}, u32[]{:S(2)}, u32[]{:S(2)}) collective-permute-start(bf16[6208,256]{1,0:T(8,128)(2,1)} %bitcast.9), channel_id=1, source_target_pairs={{0,1},{1,0},{2,3},{3,2},{4,5},{5,4},{6,7},{7,6},{8,9},{9,8},{10,11... | collective-permute-start | bytes 9535496 | tf_op jit(solution)/shard_map/ppermute | solution.py:225
  8.8 8.5 %all-to-all-start = ((bf16[8,8,512]{2,1,0:T(8,128)(2,1)}), bf16[8,8,512]{2,1,0:T(8,128)(2,1)S(1)}, u32[]{:S(2)}, u32[]{:S(2)}) async-start(bf16[8,8,512]{2,1,0:T(8,128)(2,1)} %bitcast.14), calls=%async_computation | async-start | bytes 131072 | tf_op jit(solution)/shard_map/all_to_all | solution.py:227
  12.2 0.7 copy-start.4
  12.8 0.7 copy-start.5
  13.5 3.8 %copy-start = (bf16[256,6208]{0,1:T(8,128)(2,1)S(1)}, bf16[256,6208]{0,1:T(8,128)(2,1)}, u32[]{:S(2)}) copy-start(bf16[256,6208]{0,1:T(8,128)(2,1)} %param.8) | copy-start | bytes 9535492
  17.3 25.1 %copy-start.2 = (f32[4,4096]{1,0:T(4,128)S(1)}, f32[4,4096]{1,0:T(4,128)}, u32[]{:S(2)}) copy-start(f32[4,4096]{1,0:T(4,128)} %taps_ref.1) | copy-start | bytes 196612
  17.3 25.1 %copy-start.3 = (f32[3,64]{1,0:T(4,128)S(1)}, f32[3,64]{1,0:T(4,128)}, u32[]{:S(2)}) copy-start(f32[3,64]{1,0:T(4,128)} %params.1) | copy-start | bytes 2308
  21.8 35.4 %copy-start.1 = (bf16[2048,256]{1,0:T(8,128)(2,1)S(1)}, bf16[2048,256]{1,0:T(8,128)(2,1)}, u32[]{:S(2)}) copy-start(bf16[2048,256]{1,0:T(8,128)(2,1)} %weight.1) | copy-start | bytes 3145732

commit v3 on v2

v3 whole, which is shorter than its diff:
```python
import functools

import jax
import jax.numpy as jnp
from jax import lax
from jax.experimental import pallas as pl
from jax.experimental.pallas import tpu as pltpu
from jax.sharding import PartitionSpec as P

D = 4096
HEADS = 64
HEAD_DIM = 32
GROUPS = 8
STATE = 128
SEQ = 128
INNER = HEADS * HEAD_DIM
WIDTH_BC = GROUPS * STATE
COLS = 2 * INNER + 2 * WIDTH_BC + HEADS
MEMBERS = 16
CHIPS = MEMBERS // 2
ROWS = D // MEMBERS
HALF = SEQ // 2
PER_GROUP = HEADS // GROUPS
LOCAL = HEADS // MEMBERS
CHANNELS = LOCAL * HEAD_DIM
DT_ROWS = 16
PACKED = 2 * CHANNELS + DT_ROWS

epsilon = 1e-05
F32 = jnp.float32
BF16 = jnp.bfloat16

NT = (((1,), (1,)), ((), ()))


CORE_SWAP = [(member, member ^ 1) for member in range(MEMBERS)]
CHIP_GROUPS = [[2 * chip + core for chip in range(CHIPS)] for core in range(2)]
ORDER, STARTS = 0, HEADS


def arrange_kernel(arrange):
    source = lax.broadcasted_iota(jnp.int32, (2 * SEQ, 2 * SEQ), 0)
    target = lax.broadcasted_iota(jnp.int32, (2 * SEQ, 2 * SEQ), 1)
    column = source % HALF
    token = 16 * (column // 8) + 8 * (source // SEQ) + column % 8
    wanted = token + SEQ * ((source // HALF) % 2)
    arrange[...] = jnp.where(wanted == target, 1.0, 0.0).astype(BF16)


def slot_of(member):
    return (2 * (member // 4) + member % 2) * 2 + (member // 2) % 2


def project_kernel(packing, head_group, acts, own, peer, _, out, plan, steps_ref, sorted_ref):
    begin = jnp.int32(0)
    for place in range(5):
        number = packing[place]
        plan[STARTS + number] = begin
        begin = begin + jnp.where(number < 2, INNER, jnp.where(number < 4, WIDTH_BC, HEADS))
    for spare in range(STARTS + 5, 80):
        plan[spare] = 0
    filled = jnp.int32(0)
    for head in range(HEADS):
        group = head_group[head]
        position = lax.shift_right_logical(filled, 4 * group) & 15
        plan[ORDER + group * PER_GROUP + position] = head
        filled = filled + lax.shift_left(jnp.int32(1), 4 * group)

    rows = acts[...]
    is_first = lax.axis_index("tensor") % 2 == 0
    first, second = rows[:, :ROWS], rows[:, ROWS:]
    both = jnp.concatenate(
        [jnp.where(is_first, first, second), jnp.where(is_first, second, first)], axis=1
    )
    both = jnp.concatenate([both, both], axis=0).astype(F32).T.astype(BF16)
    low = lax.broadcasted_iota(jnp.int32, (CHANNELS, SEQ), 1) < HALF

    def taken(number, begin, extent):
        where = pl.ds(pl.multiple_of(plan[STARTS + number] + begin, HEAD_DIM), extent)
        return jnp.concatenate([own[where, :], peer[where, :]], axis=1)

    for group in range(GROUPS):
        heads = [plan[ORDER + group * PER_GROUP + offset] for offset in range(PER_GROUP)]
        weights = jnp.concatenate(
            [taken(number, head * HEAD_DIM, HEAD_DIM) for number in range(2) for head in heads]
            + [taken(number, group * STATE, STATE) for number in range(2, 4)],
            axis=0,
        )
        parts = jnp.dot(weights, both, preferred_element_type=F32)
        for side in range(2):
            target = 4 * (group // 2) + 2 * side + group % 2
            for number in range(2):
                begin = (2 * number + side) * CHANNELS
                other = (4 + number) * CHANNELS
                out[target, number * CHANNELS : (number + 1) * CHANNELS, :] = jnp.where(
                    low, parts[begin : begin + CHANNELS], parts[other : other + CHANNELS]
                ).astype(BF16)

    steps_ref[...] = jnp.dot(taken(4, 0, HEADS), both, preferred_element_type=F32)
    sorted_ref[...] = jnp.zeros_like(sorted_ref)
    for member in range(MEMBERS):
        for r in range(LOCAL):
            sorted_ref[pl.ds(member * DT_ROWS + r, 1), :] = steps_ref[
                pl.ds(plan[ORDER + slot_of(member) * LOCAL + r], 1), :
            ]
    out[:, 2 * CHANNELS :, :] = sorted_ref[...].astype(BF16).reshape(MEMBERS, DT_ROWS, SEQ)


def silu(values):
    return values / (1.0 + jnp.exp(-values))


def mix_kernel(plan, params, received, taps_ref, arrange, swapped, out, held, taps_scratch, arrived):
    fetch = pltpu.make_async_copy(swapped, held, arrived)
    fetch.start()
    member = lax.axis_index("tensor")
    slot = slot_of(member)
    group = slot // 2
    heads = [plan[ORDER + slot * LOCAL + r] for r in range(LOCAL)]

    halves = []
    for core in range(2):
        total = received[core].astype(F32)
        for chip in range(1, CHIPS):
            total = total + received[2 * chip + core].astype(F32)
        halves.append(total)
    lane = lax.broadcasted_iota(jnp.int32, (1, SEQ), 1)
    summed = jnp.concatenate([half.astype(BF16) for half in halves], axis=1)
    ordered = jnp.dot(summed, arrange[...], preferred_element_type=F32)
    zx = ordered[: 2 * CHANNELS, :SEQ]
    bc = ordered[: 2 * CHANNELS, SEQ:]
    steps_raw = ordered[2 * CHANNELS :, :SEQ]

    chunks = [
        taps_ref[:, pl.ds(pl.multiple_of((heads[r] // 4) * 128, 128), 128)] for r in range(LOCAL)
    ]
    for base in (INNER, INNER + WIDTH_BC):
        chunks.append(taps_ref[:, pl.ds(pl.multiple_of(base + group * STATE, 128), 128)])
    chunks.append(jnp.zeros((128 - 4 * len(chunks), 128), F32))
    taps_scratch[...] = jnp.concatenate(chunks, axis=0).T

    def conv(values, taps):
        total = taps[:, 3:4] * values
        for tap in range(3):
            shift = 3 - tap
            moved = jnp.where(lane >= shift, pltpu.roll(values, shift, 1), 0.0)
            total = total + taps[:, tap : tap + 1] * moved
        return silu(total).astype(BF16)

    x_taps = jnp.concatenate(
        [
            taps_scratch[pl.ds(pl.multiple_of((heads[r] % 4) * HEAD_DIM, HEAD_DIM), HEAD_DIM), :][
                :, 4 * r : 4 * r + 4
            ]
            for r in range(LOCAL)
        ],
        axis=0,
    )
    x_values = conv(zx[CHANNELS:], x_taps)
    b_values = conv(bc[:CHANNELS], taps_scratch[:, 4 * LOCAL : 4 * LOCAL + 4])
    c_values = conv(bc[CHANNELS:], taps_scratch[:, 4 * LOCAL + 4 : 4 * LOCAL + 8])

    row = lax.broadcasted_iota(jnp.int32, (2 * LOCAL, SEQ), 0)

    def per_head(number):
        values = jnp.zeros((2 * LOCAL, SEQ), F32)
        for r in range(LOCAL):
            values = jnp.where(row == r, params[number, heads[r]], values)
        return values

    raw = steps_raw[: 2 * LOCAL] + per_head(0)
    steps = jnp.maximum(raw, 0.0) + jnp.log1p(jnp.exp(-jnp.abs(raw)))
    rates = -steps * jnp.exp(per_head(1))
    high = rates.astype(BF16)
    rest = rates - high.astype(F32)
    middle = rest.astype(BF16)
    low = (rest - middle.astype(F32)).astype(BF16)
    source = lax.broadcasted_iota(jnp.int32, (SEQ, SEQ), 0)
    target = lax.broadcasted_iota(jnp.int32, (SEQ, SEQ), 1)
    causal = source <= target
    until = jnp.where(causal, 1.0, 0.0).astype(BF16)
    parts = jnp.dot(jnp.concatenate([high, middle, low, low], axis=0), until, preferred_element_type=F32)
    running = parts[:8] + parts[8:16] + parts[16:24]
    columns = jnp.concatenate(
        [running[:LOCAL], steps[:LOCAL], jnp.zeros((128 - 2 * LOCAL, SEQ), F32)], axis=0
    ).T

    scores = lax.dot_general(
        b_values.astype(F32).T.astype(BF16), c_values, (((1,), (0,)), ((), ())),
        preferred_element_type=F32,
    )
    gate = silu(zx[:CHANNELS])
    mixed = []
    for r in range(LOCAL):
        spread = running[r : r + 1] - columns[:, r : r + 1]
        decay = jnp.exp(jnp.where(causal, spread, -1e30))
        weights = (decay * scores * columns[:, LOCAL + r : LOCAL + r + 1]).astype(BF16)
        x_head = x_values[r * HEAD_DIM : (r + 1) * HEAD_DIM]
        y_head = jnp.dot(x_head, weights, preferred_element_type=F32)
        mixed.append(y_head + params[2, heads[r]] * x_head.astype(F32))
    gated = jnp.concatenate(mixed, axis=0) * gate
    result = gated.T.astype(BF16)
    for index in range(CHIPS):
        out[index] = result
    fetch.wait()


def finish_kernel(plan, gathered, own, peer, out):
    core = lax.axis_index("tensor") % 2
    normed, begins = [], []
    for row in range(4):
        values = jnp.concatenate([gathered[2 * row], gathered[2 * row + 1]], axis=1).astype(F32)
        mean_square = jnp.sum(values * values, axis=1, keepdims=True) / (PER_GROUP * HEAD_DIM)
        normed.append((values * lax.rsqrt(mean_square + epsilon)).astype(BF16))
        for offset in range(PER_GROUP):
            begins.append(plan[ORDER + (2 * row + core) * PER_GROUP + offset] * HEAD_DIM)
    normed = jnp.concatenate(normed, axis=1)

    def columns(ref, place):
        rows = [ref[pl.ds(pl.multiple_of(begin, HEAD_DIM), HEAD_DIM), :] for begin in begins]
        product = jnp.dot(normed, jnp.concatenate(rows, axis=0), preferred_element_type=F32)
        out[:, :, pl.ds(pl.multiple_of(place * ROWS, ROWS), ROWS)] = product.astype(BF16).reshape(
            MEMBERS, SEQ // MEMBERS, ROWS
        )

    columns(own, core)
    columns(peer, 1 - core)


def combine_kernel(received, out):
    for chip in range(CHIPS):
        total = received[2 * chip].astype(F32) + received[2 * chip + 1].astype(F32)
        out[:, 2 * chip * ROWS : (2 * chip + 2) * ROWS] = total.astype(BF16)


SMEM = pl.BlockSpec(memory_space=pltpu.SMEM)
VMEM = pl.BlockSpec(memory_space=pltpu.VMEM)


def shards(hidden, in_weight, out_weight, conv_weight, head_params, packing, head_group):
    own = in_weight.T
    peer = lax.ppermute(own, "tensor", CORE_SWAP)
    per_chip = hidden.reshape(SEQ // MEMBERS, CHIPS, 2 * ROWS).transpose(1, 0, 2)
    acts = lax.all_to_all(
        per_chip, "tensor", split_axis=0, concat_axis=0, tiled=True, axis_index_groups=CHIP_GROUPS
    ).reshape(HALF, 2 * ROWS)

    arrange = pl.pallas_call(
        arrange_kernel,
        out_shape=jax.ShapeDtypeStruct((2 * SEQ, 2 * SEQ), BF16),
        out_specs=VMEM,
        compiler_params=pltpu.CompilerParams(vmem_limit_bytes=2 * 1024 * 1024),
        cost_estimate=pl.CostEstimate(flops=12 * 10**9, bytes_accessed=4 * 10**6, transcendentals=0),
        name="arrange",
    )()
    swapped = lax.ppermute(out_weight, "tensor", CORE_SWAP)

    partial, plan = pl.pallas_call(
        project_kernel,
        out_shape=(
            jax.ShapeDtypeStruct((MEMBERS, PACKED, SEQ), BF16),
            jax.ShapeDtypeStruct((80,), jnp.int32),
        ),
        in_specs=[SMEM, SMEM, VMEM, VMEM, VMEM, pl.BlockSpec(memory_space=pl.ANY)],
        out_specs=(VMEM, SMEM),
        scratch_shapes=[pltpu.VMEM((HEADS, SEQ), F32), pltpu.VMEM((MEMBERS * DT_ROWS, SEQ), F32)],
        compiler_params=pltpu.CompilerParams(vmem_limit_bytes=16 * 1024 * 1024),
        name="project",
    )(packing, head_group, acts, own, peer, arrange)
    partial, swapped = lax.optimization_barrier((partial, swapped))
    received = lax.all_to_all(partial, "tensor", split_axis=0, concat_axis=0, tiled=True)

    gated, held = pl.pallas_call(
        mix_kernel,
        out_shape=(
            jax.ShapeDtypeStruct((CHIPS, SEQ, CHANNELS), BF16),
            jax.ShapeDtypeStruct((INNER, ROWS), BF16),
        ),
        in_specs=[SMEM, SMEM, VMEM, VMEM, VMEM, pl.BlockSpec(memory_space=pl.ANY)],
        out_specs=(VMEM, VMEM),
        scratch_shapes=[pltpu.VMEM((128, 128), F32), pltpu.SemaphoreType.DMA(())],
        compiler_params=pltpu.CompilerParams(vmem_limit_bytes=8 * 1024 * 1024),
        name="mix",
    )(plan, head_params, received, conv_weight, arrange, swapped)
    gathered = lax.all_to_all(
        gated, "tensor", split_axis=0, concat_axis=0, tiled=True, axis_index_groups=CHIP_GROUPS
    )

    share = pl.pallas_call(
        finish_kernel,
        out_shape=jax.ShapeDtypeStruct((MEMBERS, SEQ // MEMBERS, 2 * ROWS), BF16),
        in_specs=[SMEM, VMEM, VMEM, VMEM],
        out_specs=VMEM,
        compiler_params=pltpu.CompilerParams(vmem_limit_bytes=8 * 1024 * 1024),
        name="finish",
    )(plan, gathered, out_weight, held)
    pieces = lax.all_to_all(share, "tensor", split_axis=0, concat_axis=0, tiled=True)
    return pl.pallas_call(
        combine_kernel,
        out_shape=jax.ShapeDtypeStruct((SEQ // MEMBERS, D), BF16),
        in_specs=[VMEM],
        out_specs=VMEM,
        compiler_params=pltpu.CompilerParams(vmem_limit_bytes=4 * 1024 * 1024),
        name="combine",
    )(pieces)


def solution(mesh):
    in_specs = (P(("dp", "tensor"), None), P("tensor", None), P(None, "tensor"), P(), P(), P(), P())
    out_specs = P(("dp", "tensor"), None)
    return jax.shard_map(shards, mesh=mesh, in_specs=in_specs, out_specs=out_specs, check_vma=False)
```

time: 68.5 us -> 65.5 us (0.956)
  blocking collectives: 42.8 us -> 39.9 us
  starting transfers between devices: 12.1 us -> 14.3 us
  local copies, waits for them, and re-layouts: 1.95 us -> 0.04 us
  Pallas kernels: 8.81 us -> 7.92 us
    all_to_all x2, blocking collectives: 22.2 us -> 19.3 us  [the longest x1 9.96 us: shards(): lax.all_to_all(share, 'tensor', split_axis=0, concat_axis=0, tiled=True)]
    ppermute x1 -> x2, starting transfers between devices: 8.78 us -> 11 us  [the longest x1 8.78 us: shards(): peer = lax.ppermute(own, 'tensor', CORE_SWAP)]
    unnamed x13 -> x12, local copies, waits for them, and re-layouts: 1.95 us -> 0.04 us
    pallas_call x4 -> x5, Pallas kernels: 8.81 us -> 7.92 us  [the longest x1 4.28 us: shards(): pl.pallas_call(project_kernel, out_shape=(jax.ShapeDtypeStruct((MEMBERS,...]
  transfers between devices with their start and end apart: 2 -> 3, of which waited for: 1 -> 1; matrix products, arithmetic and copies ran while one was open for 0% -> 0% of each run, Pallas kernels for 2% -> 7%
where the time goes in v3:
time: 65.5 us; the launch traced here: 65.1 us
  blocking collectives  39.9 us (61%)
  starting transfers between devices  14.3 us (22%)
  Pallas kernels  7.92 us (12%)
  waiting for transfers between devices  2.8 us (4%)
    all_to_all x1, blocking collectives, shards(): lax.all_to_all(partial, 'tensor', split_axis=0, concat_axis=0, tiled=True)  20.6 us
    all_to_all x1, blocking collectives, shards(): lax.all_to_all(share, 'tensor', split_axis=0, concat_axis=0, tiled=True)  9.96 us
    all_to_all x1, blocking collectives, shards(): lax.all_to_all(gated, 'tensor', split_axis=0, concat_axis=0, tiled=True,...  9.36 us
    ppermute x1, starting transfers between devices, shards(): peer = lax.ppermute(own, 'tensor', CORE_SWAP)  8.78 us
    pallas_call x1, Pallas kernels, shards(): pl.pallas_call(project_kernel, out_shape=(jax.ShapeDtypeStruct((MEMBERS,...  4.28 us
    all_to_all x1, starting transfers between devices, shards(): lax.all_to_all(per_chip, 'tensor', split_axis=0, concat_axis=0, tiled=Tru...  3.36 us
    all_to_all x1, waiting for transfers between devices, shards(): lax.all_to_all(per_chip, 'tensor', split_axis=0, concat_axis=0, tiled=Tru...  2.8 us
    ppermute x1, starting transfers between devices, shards(): swapped = lax.ppermute(out_weight, 'tensor', CORE_SWAP)  2.19 us
  transfers between devices with their start and end apart: 3, of which 1 were waited for; matrix products, arithmetic and copies ran while one was open for 0% of the time, Pallas kernels for 7%

profile of v3, /device:TPU:1, one launch (start us, length us, event | category | flops | bytes accessed | tf_op | source)
XLA Modules:
  0.0 65.1 jit_solution(9732678608751971743)
XLA Ops:
  0.0 8.8 %collective-permute-start = (bf16[6208,256]{1,0:T(8,128)(2,1)}, bf16[6208,256]{1,0:T(8,128)(2,1)}, u32[]{:S(2)}, u32[]{:S(2)}) collective-permute-start(bf16[6208,256]{1,0:T(8,128)(2,1)} %bitcast.5), channel_id=1, source_target_pairs={{0,1},{1,0},{2,3},{3,2},{4,5},{5,4},{6,7},{7,6},{8,9},{9,8},{10,11... | collective-permute-start | bytes 9535496 | tf_op jit(solution)/shard_map/ppermute | solution.py:242
  8.8 3.4 %all-to-all-start = ((bf16[8,8,512]{2,1,0:T(8,128)(2,1)}), bf16[8,8,512]{2,1,0:T(8,128)(2,1)S(1)}, u32[]{:S(2)}, u32[]{:S(2)}) async-start(bf16[8,8,512]{2,1,0:T(8,128)(2,1)} %bitcast.8), calls=%async_computation | async-start | bytes 131072 | tf_op jit(solution)/shard_map/all_to_all | solution.py:244
  12.2 0.0 copy-start
  12.2 0.0 copy-start.4
  12.2 0.0 copy-start.5
  12.2 2.2 %collective-permute-start.1 = (bf16[2048,256]{1,0:T(8,128)(2,1)}, bf16[2048,256]{1,0:T(8,128)(2,1)}, u32[]{:S(2)}, u32[]{:S(2)}) collective-permute-start(bf16[2048,256]{1,0:T(8,128)(2,1)} %own.1), channel_id=1, source_target_pairs={{0,1},{1,0},{2,3},{3,2},{4,5},{5,4},{6,7},{7,6},{8,9},{9,8},{10,11... | collective-permute-start | bytes 3145736 | tf_op jit(solution)/shard_map/ppermute | solution.py:256
  14.4 0.1 arrange.1._
  14.5 2.8 %all-to-all-done = bf16[8,8,512]{2,1,0:T(8,128)(2,1)S(1)} async-done(((bf16[8,8,512]{2,1,0:T(8,128)(2,1)}), bf16[8,8,512]{2,1,0:T(8,128)(2,1)S(1)}, u32[]{:S(2)}, u32[]{:S(2)}) %all-to-all-start) | async-done | bytes 65568 | tf_op jit(solution)/shard_map/all_to_all | solution.py:244
  17.3 0.0 collective-permute-done.peer
  17.3 0.0 copy-done
  17.3 0.0 copy-done.4
  17.3 0.0 copy-done.5
  17.3 0.0 copy-start.2
  17.3 0.0 copy-start.3
  17.3 4.3 %project.1 = (bf16[16,272,128]{2,1,0:T(8,128)(2,1)S(1)}, s32[80]{0:T(128)S(1)}) custom-call(s32[5]{0:T(128)S(1)} %copy-done.4, s32[64]{0:T(128)S(1)} %copy-done.5, bf16[64,512]{1,0:T(8,128)(2,1)S(1)} %bitcast.7, bf16[6208,256]{1,0:T(8,128)(2,1)S(1)} %bitcast.6, bf16[6208,256]{1,0:T(8,128)(2,1)} %collective-permute-done.peer, bf16[256,256]{1,0:T(8,128)(2,1)S(1)} %arrange.1._), custom_call_target="tpu_custom_call" | custom-call | tf_op jit(solution)/shard_map/project/pallas_call | solution.py:258
  21.6 0.0 copy-start.1
  21.6 0.0 collective-permute-done.1.swapped
  21.6 20.6 %all_to_all.20.received = bf16[16,272,128]{2,1,0:T(8,128)(2,1)S(1)} all-to-all(bf16[16,272,128]{2,1,0:T(8,128)(2,1)S(1)} %get-tuple-element.13), channel_id=1, replica_groups=mesh['dp'=32,'tensor'=16] {'tensor'}, dimensions={0} | all-to-all | bytes 2228224 | tf_op jit(solution)/shard_map/all_to_all | solution.py:271
  42.3 0.0 copy-done.2
  42.3 2.0 %mix.1 = (bf16[8,128,128]{2,1,0:T(8,128)(2,1)S(1)}, bf16[2048,256]{1,0:T(8,128)(2,1)S(1)}) custom-call(s32[80]{0:T(128)S(1)} %get-tuple-element.11.plan, f32[3,64]{1,0:T(4,128)S(1)} %copy-done.3, bf16[16,272,128]{2,1,0:T(8,128)(2,1)S(1)} %all_to_all.20.received, f32[4,4096]{1,0:T(4,128)S(1)} %copy-done.2, bf16[256,256]{1,0:T(8,128)(2,1)S(1)} %arrange.1._, ...), custom_call_target="tpu_custom_call" | custom-call | tf_op jit(solution)/shard_map/mix/pallas_call | solution.py:273
  44.3 9.4 %all_to_all.21.gathered = bf16[8,128,128]{2,1,0:T(8,128)(2,1)S(1)} all-to-all(bf16[8,128,128]{2,1,0:T(8,128)(2,1)S(1)} %get-tuple-element.15), channel_id=1, replica_groups={{0,2,4,6,8,10,12,14},{1,3,5,7,9,11,13,15},{16,18,20,22,24,26,28,30},{17..., dimensions={0} | all-to-all | bytes 524288 | tf_op jit(solution)/shard_map/all_to_all | solution.py:285
  53.6 0.9 %finish.1 = bf16[16,8,512]{2,1,0:T(8,128)(2,1)S(1)} custom-call(s32[80]{0:T(128)S(1)} %get-tuple-element.11.plan, bf16[8,128,128]{2,1,0:T(8,128)(2,1)S(1)} %all_to_all.21.gathered, bf16[2048,256]{1,0:T(8,128)(2,1)S(1)} %copy-done.1, bf16[2048,256]{1,0:T(8,128)(2,1)S(1)} %get-tuple-element.16.peer), custom_call_target="tpu_custom_call" | custom-call | tf_op jit(solution)/shard_map/finish/pallas_call | solution.py:289
  54.5 10.0 %all_to_all.22.received = bf16[16,8,512]{2,1,0:T(8,128)(2,1)S(1)} all-to-all(bf16[16,8,512]{2,1,0:T(8,128)(2,1)S(1)} %finish.1), channel_id=1, replica_groups=mesh['dp'=32,'tensor'=16] {'tensor'}, dimensions={0} | all-to-all | bytes 262144 | tf_op jit(solution)/shard_map/all_to_all | solution.py:297
  64.5 0.6 combine.1
  (2 shorter events, 0.0 us)
Async XLA Ops:
  0.0 17.3 %collective-permute-start = (bf16[6208,256]{1,0:T(8,128)(2,1)}, bf16[6208,256]{1,0:T(8,128)(2,1)}, u32[]{:S(2)}, u32[]{:S(2)}) collective-permute-start(bf16[6208,256]{1,0:T(8,128)(2,1)} %bitcast.5), channel_id=1, source_target_pairs={{0,1},{1,0},{2,3},{3,2},{4,5},{5,4},{6,7},{7,6},{8,9},{9,8},{10,11... | collective-permute-start | bytes 9535496 | tf_op jit(solution)/shard_map/ppermute | solution.py:242
  8.8 8.5 %all-to-all-start = ((bf16[8,8,512]{2,1,0:T(8,128)(2,1)}), bf16[8,8,512]{2,1,0:T(8,128)(2,1)S(1)}, u32[]{:S(2)}, u32[]{:S(2)}) async-start(bf16[8,8,512]{2,1,0:T(8,128)(2,1)} %bitcast.8), calls=%async_computation | async-start | bytes 131072 | tf_op jit(solution)/shard_map/all_to_all | solution.py:244
  12.2 5.1 %copy-start = (bf16[256,6208]{0,1:T(8,128)(2,1)S(1)}, bf16[256,6208]{0,1:T(8,128)(2,1)}, u32[]{:S(2)}) copy-start(bf16[256,6208]{0,1:T(8,128)(2,1)} %param.8) | copy-start | bytes 9535492
  12.2 5.1 %copy-start.4 = (s32[5]{0:T(128)S(1)}, s32[5]{0:T(128)}, u32[]{:S(2)}) copy-start(s32[5]{0:T(128)} %packing.1) | copy-start | bytes 64
  12.2 5.1 %copy-start.5 = (s32[64]{0:T(128)S(1)}, s32[64]{0:T(128)}, u32[]{:S(2)}) copy-start(s32[64]{0:T(128)} %head_group.1) | copy-start | bytes 772
  12.2 9.4 %collective-permute-start.1 = (bf16[2048,256]{1,0:T(8,128)(2,1)}, bf16[2048,256]{1,0:T(8,128)(2,1)}, u32[]{:S(2)}, u32[]{:S(2)}) collective-permute-start(bf16[2048,256]{1,0:T(8,128)(2,1)} %own.1), channel_id=1, source_target_pairs={{0,1},{1,0},{2,3},{3,2},{4,5},{5,4},{6,7},{7,6},{8,9},{9,8},{10,11... | collective-permute-start | bytes 3145736 | tf_op jit(solution)/shard_map/ppermute | solution.py:256
  17.3 25.0 %copy-start.2 = (f32[4,4096]{1,0:T(4,128)S(1)}, f32[4,4096]{1,0:T(4,128)}, u32[]{:S(2)}) copy-start(f32[4,4096]{1,0:T(4,128)} %taps_ref.1) | copy-start | bytes 196612
  17.3 25.0 %copy-start.3 = (f32[3,64]{1,0:T(4,128)S(1)}, f32[3,64]{1,0:T(4,128)}, u32[]{:S(2)}) copy-start(f32[3,64]{1,0:T(4,128)} %params.1) | copy-start | bytes 2308
  21.6 32.0 %copy-start.1 = (bf16[2048,256]{1,0:T(8,128)(2,1)S(1)}, bf16[2048,256]{1,0:T(8,128)(2,1)}, u32[]{:S(2)}) copy-start(bf16[2048,256]{1,0:T(8,128)(2,1)} %own.1) | copy-start | bytes 3145732

commit v4 on v3

--- a/solution.py
+++ b/solution.py
@@ -110,13 +110,19 @@
     return values / (1.0 + jnp.exp(-values))
 
 
-def mix_kernel(plan, params, received, taps_ref, arrange, swapped, out, held, taps_scratch, arrived):
-    fetch = pltpu.make_async_copy(swapped, held, arrived)
-    fetch.start()
+def mix_kernel(
+    plan_ref, params_ref, received, taps_ref, arrange, swapped, out, held, taps_scratch, plan, params, arrived
+):
+    scalars = [
+        pltpu.make_async_copy(plan_ref, plan, arrived.at[0]),
+        pltpu.make_async_copy(params_ref, params, arrived.at[1]),
+    ]
+    fetch = pltpu.make_async_copy(swapped, held, arrived.at[2])
+    for copy in (*scalars, fetch):
+        copy.start()
     member = lax.axis_index("tensor")
     slot = slot_of(member)
     group = slot // 2
-    heads = [plan[ORDER + slot * LOCAL + r] for r in range(LOCAL)]
 
     halves = []
     for core in range(2):
@@ -131,13 +137,16 @@
     bc = ordered[: 2 * CHANNELS, SEQ:]
     steps_raw = ordered[2 * CHANNELS :, :SEQ]
 
-    chunks = [
-        taps_ref[:, pl.ds(pl.multiple_of((heads[r] // 4) * 128, 128), 128)] for r in range(LOCAL)
-    ]
-    for base in (INNER, INNER + WIDTH_BC):
-        chunks.append(taps_ref[:, pl.ds(pl.multiple_of(base + group * STATE, 128), 128)])
-    chunks.append(jnp.zeros((128 - 4 * len(chunks), 128), F32))
-    taps_scratch[...] = jnp.concatenate(chunks, axis=0).T
+    def columns_of(chunks):
+        filler = jnp.zeros((128 - 4 * len(chunks), 128), F32)
+        return jnp.concatenate(chunks + [filler], axis=0).T
+
+    state_taps = columns_of(
+        [
+            taps_ref[:, pl.ds(pl.multiple_of(base + group * STATE, 128), 128)]
+            for base in (INNER, INNER + WIDTH_BC)
+        ]
+    )
 
     def conv(values, taps):
         total = taps[:, 3:4] * values
@@ -147,6 +156,20 @@
             total = total + taps[:, tap : tap + 1] * moved
         return silu(total).astype(BF16)
 
+    b_values = conv(bc[:CHANNELS], state_taps[:, :4])
+    c_values = conv(bc[CHANNELS:], state_taps[:, 4:8])
+    scores = lax.dot_general(
+        b_values.astype(F32).T.astype(BF16), c_values, (((1,), (0,)), ((), ())),
+        preferred_element_type=F32,
+    )
+    gate = silu(zx[:CHANNELS])
+
+    for copy in scalars:
+        copy.wait()
+    heads = [plan[ORDER + slot * LOCAL + r] for r in range(LOCAL)]
+    taps_scratch[...] = columns_of(
+        [taps_ref[:, pl.ds(pl.multiple_of((head // 4) * 128, 128), 128)] for head in heads]
+    )
     x_taps = jnp.concatenate(
         [
             taps_scratch[pl.ds(pl.multiple_of((heads[r] % 4) * HEAD_DIM, HEAD_DIM), HEAD_DIM), :][
@@ -157,8 +180,6 @@
         axis=0,
     )
     x_values = conv(zx[CHANNELS:], x_taps)
-    b_values = conv(bc[:CHANNELS], taps_scratch[:, 4 * LOCAL : 4 * LOCAL + 4])
-    c_values = conv(bc[CHANNELS:], taps_scratch[:, 4 * LOCAL + 4 : 4 * LOCAL + 8])
 
     row = lax.broadcasted_iota(jnp.int32, (2 * LOCAL, SEQ), 0)
 
@@ -185,11 +206,6 @@
         [running[:LOCAL], steps[:LOCAL], jnp.zeros((128 - 2 * LOCAL, SEQ), F32)], axis=0
     ).T
 
-    scores = lax.dot_general(
-        b_values.astype(F32).T.astype(BF16), c_values, (((1,), (0,)), ((), ())),
-        preferred_element_type=F32,
-    )
-    gate = silu(zx[:CHANNELS])
     mixed = []
     for r in range(LOCAL):
         spread = running[r : r + 1] - columns[:, r : r + 1]
@@ -205,16 +221,22 @@
     fetch.wait()
 
 
-def finish_kernel(plan, gathered, own, peer, out):
+def finish_kernel(plan_ref, gathered, own, peer, out, plan, arrived):
+    fetch = pltpu.make_async_copy(plan_ref, plan, arrived)
+    fetch.start()
     core = lax.axis_index("tensor") % 2
-    normed, begins = [], []
+    normed = []
     for row in range(4):
         values = jnp.concatenate([gathered[2 * row], gathered[2 * row + 1]], axis=1).astype(F32)
         mean_square = jnp.sum(values * values, axis=1, keepdims=True) / (PER_GROUP * HEAD_DIM)
         normed.append((values * lax.rsqrt(mean_square + epsilon)).astype(BF16))
-        for offset in range(PER_GROUP):
-            begins.append(plan[ORDER + (2 * row + core) * PER_GROUP + offset] * HEAD_DIM)
     normed = jnp.concatenate(normed, axis=1)
+    fetch.wait()
+    begins = [
+        plan[ORDER + (2 * row + core) * PER_GROUP + offset] * HEAD_DIM
+        for row in range(4)
+        for offset in range(PER_GROUP)
+    ]
 
     def columns(ref, place):
         rows = [ref[pl.ds(pl.multiple_of(begin, HEAD_DIM), HEAD_DIM), :] for begin in begins]
@@ -235,6 +257,7 @@
 
 SMEM = pl.BlockSpec(memory_space=pltpu.SMEM)
 VMEM = pl.BlockSpec(memory_space=pltpu.VMEM)
+ANY = pl.BlockSpec(memory_space=pl.ANY)
 
 
 def shards(hidden, in_weight, out_weight, conv_weight, head_params, packing, head_group):
@@ -276,9 +299,14 @@
             jax.ShapeDtypeStruct((CHIPS, SEQ, CHANNELS), BF16),
             jax.ShapeDtypeStruct((INNER, ROWS), BF16),
         ),
-        in_specs=[SMEM, SMEM, VMEM, VMEM, VMEM, pl.BlockSpec(memory_space=pl.ANY)],
+        in_specs=[ANY, ANY, VMEM, VMEM, VMEM, ANY],
         out_specs=(VMEM, VMEM),
-        scratch_shapes=[pltpu.VMEM((128, 128), F32), pltpu.SemaphoreType.DMA(())],
+        scratch_shapes=[
+            pltpu.VMEM((128, 128), F32),
+            pltpu.SMEM((80,), jnp.int32),
+            pltpu.SMEM((3, HEADS), F32),
+            pltpu.SemaphoreType.DMA((3,)),
+        ],
         compiler_params=pltpu.CompilerParams(vmem_limit_bytes=8 * 1024 * 1024),
         name="mix",
     )(plan, head_params, received, conv_weight, arrange, swapped)
@@ -289,8 +317,9 @@
     share = pl.pallas_call(
         finish_kernel,
         out_shape=jax.ShapeDtypeStruct((MEMBERS, SEQ // MEMBERS, 2 * ROWS), BF16),
-        in_specs=[SMEM, VMEM, VMEM, VMEM],
+        in_specs=[ANY, VMEM, VMEM, VMEM],
         out_specs=VMEM,
+        scratch_shapes=[pltpu.SMEM((80,), jnp.int32), pltpu.SemaphoreType.DMA(())],
         compiler_params=pltpu.CompilerParams(vmem_limit_bytes=8 * 1024 * 1024),
         name="finish",
     )(plan, gathered, out_weight, held)

time: 65.5 us -> 65 us (level)
  no operation moved by 1% of the time
where the time goes in v4:
time: 65 us; the launch traced here: 64.7 us
  blocking collectives  39.9 us (61%)
  starting transfers between devices  14.3 us (22%)
  Pallas kernels  7.42 us (11%)
  waiting for transfers between devices  2.8 us (4%)
    all_to_all x1, blocking collectives, shards(): lax.all_to_all(partial, 'tensor', split_axis=0, concat_axis=0, tiled=True)  20.6 us
    all_to_all x1, blocking collectives, shards(): lax.all_to_all(share, 'tensor', split_axis=0, concat_axis=0, tiled=True)  9.96 us
    all_to_all x1, blocking collectives, shards(): lax.all_to_all(gated, 'tensor', split_axis=0, concat_axis=0, tiled=True,...  9.36 us
    ppermute x1, starting transfers between devices, shards(): peer = lax.ppermute(own, 'tensor', CORE_SWAP)  8.78 us
    pallas_call x1, Pallas kernels, shards(): pl.pallas_call(project_kernel, out_shape=(jax.ShapeDtypeStruct((MEMBERS,...  4.28 us
    all_to_all x1, starting transfers between devices, shards(): lax.all_to_all(per_chip, 'tensor', split_axis=0, concat_axis=0, tiled=Tru...  3.36 us
    all_to_all x1, waiting for transfers between devices, shards(): lax.all_to_all(per_chip, 'tensor', split_axis=0, concat_axis=0, tiled=Tru...  2.8 us
    ppermute x1, starting transfers between devices, shards(): swapped = lax.ppermute(out_weight, 'tensor', CORE_SWAP)  2.19 us
  transfers between devices with their start and end apart: 3, of which 1 were waited for; matrix products, arithmetic and copies ran while one was open for 0% of the time, Pallas kernels for 7%

profile of v4, /device:TPU:1, one launch (start us, length us, event | category | flops | bytes accessed | tf_op | source)
XLA Modules:
  0.0 64.7 jit_solution(8349867029254135550)
XLA Ops:
  0.0 8.8 %collective-permute-start = (bf16[6208,256]{1,0:T(8,128)(2,1)}, bf16[6208,256]{1,0:T(8,128)(2,1)}, u32[]{:S(2)}, u32[]{:S(2)}) collective-permute-start(bf16[6208,256]{1,0:T(8,128)(2,1)} %bitcast.5), channel_id=1, source_target_pairs={{0,1},{1,0},{2,3},{3,2},{4,5},{5,4},{6,7},{7,6},{8,9},{9,8},{10,11... | collective-permute-start | bytes 9535496 | tf_op jit(solution)/shard_map/ppermute | solution.py:265
  8.8 3.4 %all-to-all-start = ((bf16[8,8,512]{2,1,0:T(8,128)(2,1)}), bf16[8,8,512]{2,1,0:T(8,128)(2,1)S(1)}, u32[]{:S(2)}, u32[]{:S(2)}) async-start(bf16[8,8,512]{2,1,0:T(8,128)(2,1)} %bitcast.8), calls=%async_computation | async-start | bytes 131072 | tf_op jit(solution)/shard_map/all_to_all | solution.py:267
  12.2 0.0 copy-start
  12.2 0.0 copy-start.4
  12.2 0.0 copy-start.5
  12.2 2.2 %collective-permute-start.1 = (bf16[2048,256]{1,0:T(8,128)(2,1)}, bf16[2048,256]{1,0:T(8,128)(2,1)}, u32[]{:S(2)}, u32[]{:S(2)}) collective-permute-start(bf16[2048,256]{1,0:T(8,128)(2,1)} %own.1), channel_id=1, source_target_pairs={{0,1},{1,0},{2,3},{3,2},{4,5},{5,4},{6,7},{7,6},{8,9},{9,8},{10,11... | collective-permute-start | bytes 3145736 | tf_op jit(solution)/shard_map/ppermute | solution.py:279
  14.4 0.1 arrange.1._
  14.5 2.8 %all-to-all-done = bf16[8,8,512]{2,1,0:T(8,128)(2,1)S(1)} async-done(((bf16[8,8,512]{2,1,0:T(8,128)(2,1)}), bf16[8,8,512]{2,1,0:T(8,128)(2,1)S(1)}, u32[]{:S(2)}, u32[]{:S(2)}) %all-to-all-start) | async-done | bytes 65568 | tf_op jit(solution)/shard_map/all_to_all | solution.py:267
  17.3 0.0 collective-permute-done.peer
  17.3 0.0 copy-done
  17.3 0.0 copy-done.4
  17.3 0.0 copy-done.5
  17.3 0.0 copy-start.2
  17.3 0.0 copy-start.3
  17.3 4.3 %project.1 = (bf16[16,272,128]{2,1,0:T(8,128)(2,1)S(1)}, s32[80]{0:T(128)S(1)}) custom-call(s32[5]{0:T(128)S(1)} %copy-done.4, s32[64]{0:T(128)S(1)} %copy-done.5, bf16[64,512]{1,0:T(8,128)(2,1)S(1)} %bitcast.7, bf16[6208,256]{1,0:T(8,128)(2,1)S(1)} %bitcast.6, bf16[6208,256]{1,0:T(8,128)(2,1)} %collective-permute-done.peer, bf16[256,256]{1,0:T(8,128)(2,1)S(1)} %arrange.1._), custom_call_target="tpu_custom_call" | custom-call | tf_op jit(solution)/shard_map/project/pallas_call | solution.py:281
  21.6 0.0 copy-start.1
  21.6 0.0 collective-permute-done.1.swapped
  21.6 20.6 %all_to_all.20.received = bf16[16,272,128]{2,1,0:T(8,128)(2,1)S(1)} all-to-all(bf16[16,272,128]{2,1,0:T(8,128)(2,1)S(1)} %get-tuple-element.13), channel_id=1, replica_groups=mesh['dp'=32,'tensor'=16] {'tensor'}, dimensions={0} | all-to-all | bytes 2228224 | tf_op jit(solution)/shard_map/all_to_all | solution.py:294
  42.3 0.0 copy-done.2
  42.3 1.5 %mix.1 = (bf16[8,128,128]{2,1,0:T(8,128)(2,1)S(1)}, bf16[2048,256]{1,0:T(8,128)(2,1)S(1)}) custom-call(s32[80]{0:T(128)S(1)} %get-tuple-element.11.plan_ref, f32[3,64]{1,0:T(4,128)S(1)} %copy-done.3, bf16[16,272,128]{2,1,0:T(8,128)(2,1)S(1)} %all_to_all.20.received, f32[4,4096]{1,0:T(4,128)S(1)} %copy-done.2, bf16[256,256]{1,0:T(8,128)(2,1)S(1)} %arrange.1._, ...), custom_call_target="tpu_custom_call" | custom-call | tf_op jit(solution)/shard_map/mix/pallas_call | solution.py:296
  43.8 9.4 %all_to_all.21.gathered = bf16[8,128,128]{2,1,0:T(8,128)(2,1)S(1)} all-to-all(bf16[8,128,128]{2,1,0:T(8,128)(2,1)S(1)} %get-tuple-element.15), channel_id=1, replica_groups={{0,2,4,6,8,10,12,14},{1,3,5,7,9,11,13,15},{16,18,20,22,24,26,28,30},{17..., dimensions={0} | all-to-all | bytes 524288 | tf_op jit(solution)/shard_map/all_to_all | solution.py:313
  53.2 0.9 %finish.1 = bf16[16,8,512]{2,1,0:T(8,128)(2,1)S(1)} custom-call(s32[80]{0:T(128)S(1)} %get-tuple-element.11.plan_ref, bf16[8,128,128]{2,1,0:T(8,128)(2,1)S(1)} %all_to_all.21.gathered, bf16[2048,256]{1,0:T(8,128)(2,1)S(1)} %copy-done.1, bf16[2048,256]{1,0:T(8,128)(2,1)S(1)} %get-tuple-element.16.peer), custom_call_target="tpu_custom_call" | custom-call | tf_op jit(solution)/shard_map/finish/pallas_call | solution.py:317
  54.0 10.0 %all_to_all.22.received = bf16[16,8,512]{2,1,0:T(8,128)(2,1)S(1)} all-to-all(bf16[16,8,512]{2,1,0:T(8,128)(2,1)S(1)} %finish.1), channel_id=1, replica_groups=mesh['dp'=32,'tensor'=16] {'tensor'}, dimensions={0} | all-to-all | bytes 262144 | tf_op jit(solution)/shard_map/all_to_all | solution.py:326
  64.0 0.6 %combine.1 = bf16[8,4096]{1,0:T(8,128)(2,1)} custom-call(bf16[16,8,512]{2,1,0:T(8,128)(2,1)S(1)} %all_to_all.22.received), custom_call_target="tpu_custom_call" | custom-call | tf_op jit(solution)/shard_map/combine/pallas_call | solution.py:327
  (2 shorter events, 0.0 us)
Async XLA Ops:
  0.0 17.3 %collective-permute-start = (bf16[6208,256]{1,0:T(8,128)(2,1)}, bf16[6208,256]{1,0:T(8,128)(2,1)}, u32[]{:S(2)}, u32[]{:S(2)}) collective-permute-start(bf16[6208,256]{1,0:T(8,128)(2,1)} %bitcast.5), channel_id=1, source_target_pairs={{0,1},{1,0},{2,3},{3,2},{4,5},{5,4},{6,7},{7,6},{8,9},{9,8},{10,11... | collective-permute-start | bytes 9535496 | tf_op jit(solution)/shard_map/ppermute | solution.py:265
  8.8 8.5 %all-to-all-start = ((bf16[8,8,512]{2,1,0:T(8,128)(2,1)}), bf16[8,8,512]{2,1,0:T(8,128)(2,1)S(1)}, u32[]{:S(2)}, u32[]{:S(2)}) async-start(bf16[8,8,512]{2,1,0:T(8,128)(2,1)} %bitcast.8), calls=%async_computation | async-start | bytes 131072 | tf_op jit(solution)/shard_map/all_to_all | solution.py:267
  12.2 5.1 %copy-start = (bf16[256,6208]{0,1:T(8,128)(2,1)S(1)}, bf16[256,6208]{0,1:T(8,128)(2,1)}, u32[]{:S(2)}) copy-start(bf16[256,6208]{0,1:T(8,128)(2,1)} %param.8) | copy-start | bytes 9535492
  12.2 5.1 %copy-start.4 = (s32[5]{0:T(128)S(1)}, s32[5]{0:T(128)}, u32[]{:S(2)}) copy-start(s32[5]{0:T(128)} %packing.1) | copy-start | bytes 64
  12.2 5.1 %copy-start.5 = (s32[64]{0:T(128)S(1)}, s32[64]{0:T(128)}, u32[]{:S(2)}) copy-start(s32[64]{0:T(128)} %head_group.1) | copy-start | bytes 772
  12.2 9.4 %collective-permute-start.1 = (bf16[2048,256]{1,0:T(8,128)(2,1)}, bf16[2048,256]{1,0:T(8,128)(2,1)}, u32[]{:S(2)}, u32[]{:S(2)}) collective-permute-start(bf16[2048,256]{1,0:T(8,128)(2,1)} %own.1), channel_id=1, source_target_pairs={{0,1},{1,0},{2,3},{3,2},{4,5},{5,4},{6,7},{7,6},{8,9},{9,8},{10,11... | collective-permute-start | bytes 3145736 | tf_op jit(solution)/shard_map/ppermute | solution.py:279
  17.3 25.0 %copy-start.2 = (f32[4,4096]{1,0:T(4,128)S(1)}, f32[4,4096]{1,0:T(4,128)}, u32[]{:S(2)}) copy-start(f32[4,4096]{1,0:T(4,128)} %taps_ref.1) | copy-start | bytes 196612
  17.3 25.0 %copy-start.3 = (f32[3,64]{1,0:T(4,128)S(1)}, f32[3,64]{1,0:T(4,128)}, u32[]{:S(2)}) copy-start(f32[3,64]{1,0:T(4,128)} %params_ref.1) | copy-start | bytes 2308
  21.6 31.6 %copy-start.1 = (bf16[2048,256]{1,0:T(8,128)(2,1)S(1)}, bf16[2048,256]{1,0:T(8,128)(2,1)}, u32[]{:S(2)}) copy-start(bf16[2048,256]{1,0:T(8,128)(2,1)} %own.1) | copy-start | bytes 3145732

commit v5 on v4

--- a/solution.py
+++ b/solution.py
@@ -111,7 +111,8 @@
 
 
 def mix_kernel(
-    plan_ref, params_ref, received, taps_ref, arrange, swapped, out, held, taps_scratch, plan, params, arrived
+    plan_ref, params_ref, received, taps_ref, arrange, weight, swapped,
+    out, mine, theirs, taps_scratch, held, plan, params, arrived,
 ):
     scalars = [
         pltpu.make_async_copy(plan_ref, plan, arrived.at[0]),
@@ -218,12 +219,24 @@
     result = gated.T.astype(BF16)
     for index in range(CHIPS):
         out[index] = result
+    begins = [
+        plan[ORDER + (2 * row + member % 2) * PER_GROUP + offset] * HEAD_DIM
+        for row in range(4)
+        for offset in range(PER_GROUP)
+    ]
+
+    def sort_rows(source, sink):
+        for place, begin in enumerate(begins):
+            sink[place * HEAD_DIM : (place + 1) * HEAD_DIM, :] = source[
+                pl.ds(pl.multiple_of(begin, HEAD_DIM), HEAD_DIM), :
+            ]
+
+    sort_rows(weight, mine)
     fetch.wait()
-
-
-def finish_kernel(plan_ref, gathered, own, peer, out, plan, arrived):
-    fetch = pltpu.make_async_copy(plan_ref, plan, arrived)
-    fetch.start()
+    sort_rows(held, theirs)
+
+
+def finish_kernel(gathered, own, peer, out):
     core = lax.axis_index("tensor") % 2
     normed = []
     for row in range(4):
@@ -231,22 +244,11 @@
         mean_square = jnp.sum(values * values, axis=1, keepdims=True) / (PER_GROUP * HEAD_DIM)
         normed.append((values * lax.rsqrt(mean_square + epsilon)).astype(BF16))
     normed = jnp.concatenate(normed, axis=1)
-    fetch.wait()
-    begins = [
-        plan[ORDER + (2 * row + core) * PER_GROUP + offset] * HEAD_DIM
-        for row in range(4)
-        for offset in range(PER_GROUP)
-    ]
-
-    def columns(ref, place):
-        rows = [ref[pl.ds(pl.multiple_of(begin, HEAD_DIM), HEAD_DIM), :] for begin in begins]
-        product = jnp.dot(normed, jnp.concatenate(rows, axis=0), preferred_element_type=F32)
+    for ref, place in ((own, core), (peer, 1 - core)):
+        product = jnp.dot(normed, ref[...], preferred_element_type=F32)
         out[:, :, pl.ds(pl.multiple_of(place * ROWS, ROWS), ROWS)] = product.astype(BF16).reshape(
             MEMBERS, SEQ // MEMBERS, ROWS
         )
-
-    columns(own, core)
-    columns(peer, 1 - core)
 
 
 def combine_kernel(received, out):
@@ -293,23 +295,25 @@
     partial, swapped = lax.optimization_barrier((partial, swapped))
     received = lax.all_to_all(partial, "tensor", split_axis=0, concat_axis=0, tiled=True)
 
-    gated, held = pl.pallas_call(
+    gated, mine, theirs = pl.pallas_call(
         mix_kernel,
         out_shape=(
             jax.ShapeDtypeStruct((CHIPS, SEQ, CHANNELS), BF16),
-            jax.ShapeDtypeStruct((INNER, ROWS), BF16),
+            jax.ShapeDtypeStruct((INNER // 2, ROWS), BF16),
+            jax.ShapeDtypeStruct((INNER // 2, ROWS), BF16),
         ),
-        in_specs=[ANY, ANY, VMEM, VMEM, VMEM, ANY],
-        out_specs=(VMEM, VMEM),
+        in_specs=[ANY, ANY, VMEM, VMEM, VMEM, VMEM, ANY],
+        out_specs=(VMEM, VMEM, VMEM),
         scratch_shapes=[
             pltpu.VMEM((128, 128), F32),
+            pltpu.VMEM((INNER, ROWS), BF16),
             pltpu.SMEM((80,), jnp.int32),
             pltpu.SMEM((3, HEADS), F32),
             pltpu.SemaphoreType.DMA((3,)),
         ],
         compiler_params=pltpu.CompilerParams(vmem_limit_bytes=8 * 1024 * 1024),
         name="mix",
-    )(plan, head_params, received, conv_weight, arrange, swapped)
+    )(plan, head_params, received, conv_weight, arrange, out_weight, swapped)
     gathered = lax.all_to_all(
         gated, "tensor", split_axis=0, concat_axis=0, tiled=True, axis_index_groups=CHIP_GROUPS
     )
@@ -317,12 +321,11 @@
     share = pl.pallas_call(
         finish_kernel,
         out_shape=jax.ShapeDtypeStruct((MEMBERS, SEQ // MEMBERS, 2 * ROWS), BF16),
-        in_specs=[ANY, VMEM, VMEM, VMEM],
+        in_specs=[VMEM, VMEM, VMEM],
         out_specs=VMEM,
-        scratch_shapes=[pltpu.SMEM((80,), jnp.int32), pltpu.SemaphoreType.DMA(())],
         compiler_params=pltpu.CompilerParams(vmem_limit_bytes=8 * 1024 * 1024),
         name="finish",
-    )(plan, gathered, out_weight, held)
+    )(gathered, mine, theirs)
     pieces = lax.all_to_all(share, "tensor", split_axis=0, concat_axis=0, tiled=True)
     return pl.pallas_call(
         combine_kernel,

time: 65 us -> 64.5 us (level)
  no operation moved by 1% of the time
where the time goes in v5:
time: 64.5 us; the launch traced here: 64.1 us
  blocking collectives  39.8 us (62%)
  starting transfers between devices  14.3 us (22%)
  Pallas kernels  7.02 us (11%)
  waiting for transfers between devices  2.8 us (4%)
    all_to_all x1, blocking collectives, shards(): lax.all_to_all(partial, 'tensor', split_axis=0, concat_axis=0, tiled=True)  20.5 us
    all_to_all x1, blocking collectives, shards(): lax.all_to_all(share, 'tensor', split_axis=0, concat_axis=0, tiled=True)  9.96 us
    all_to_all x1, blocking collectives, shards(): lax.all_to_all(gated, 'tensor', split_axis=0, concat_axis=0, tiled=True,...  9.36 us
    ppermute x1, starting transfers between devices, shards(): peer = lax.ppermute(own, 'tensor', CORE_SWAP)  8.78 us
    pallas_call x1, Pallas kernels, shards(): pl.pallas_call(project_kernel, out_shape=(jax.ShapeDtypeStruct((MEMBERS,...  4.34 us
    all_to_all x1, starting transfers between devices, shards(): lax.all_to_all(per_chip, 'tensor', split_axis=0, concat_axis=0, tiled=Tru...  3.36 us
    all_to_all x1, waiting for transfers between devices, shards(): lax.all_to_all(per_chip, 'tensor', split_axis=0, concat_axis=0, tiled=Tru...  2.8 us
    ppermute x1, starting transfers between devices, shards(): swapped = lax.ppermute(out_weight, 'tensor', CORE_SWAP)  2.19 us
  transfers between devices with their start and end apart: 3, of which 1 were waited for; matrix products, arithmetic and copies ran while one was open for 0% of the time, Pallas kernels for 7%

profile of v5, /device:TPU:1, one launch (start us, length us, event | category | flops | bytes accessed | tf_op | source)
XLA Modules:
  0.0 64.1 jit_solution(16026233518698293930)
XLA Ops:
  0.0 8.8 %collective-permute-start = (bf16[6208,256]{1,0:T(8,128)(2,1)}, bf16[6208,256]{1,0:T(8,128)(2,1)}, u32[]{:S(2)}, u32[]{:S(2)}) collective-permute-start(bf16[6208,256]{1,0:T(8,128)(2,1)} %bitcast.5), channel_id=1, source_target_pairs={{0,1},{1,0},{2,3},{3,2},{4,5},{5,4},{6,7},{7,6},{8,9},{9,8},{10,11... | collective-permute-start | bytes 9535496 | tf_op jit(solution)/shard_map/ppermute | solution.py:267
  8.8 3.4 %all-to-all-start = ((bf16[8,8,512]{2,1,0:T(8,128)(2,1)}), bf16[8,8,512]{2,1,0:T(8,128)(2,1)S(1)}, u32[]{:S(2)}, u32[]{:S(2)}) async-start(bf16[8,8,512]{2,1,0:T(8,128)(2,1)} %bitcast.8), calls=%async_computation | async-start | bytes 131072 | tf_op jit(solution)/shard_map/all_to_all | solution.py:269
  12.2 0.0 copy-start
  12.2 0.0 copy-start.4
  12.2 0.0 copy-start.5
  12.2 2.2 %collective-permute-start.1 = (bf16[2048,256]{1,0:T(8,128)(2,1)}, bf16[2048,256]{1,0:T(8,128)(2,1)}, u32[]{:S(2)}, u32[]{:S(2)}) collective-permute-start(bf16[2048,256]{1,0:T(8,128)(2,1)} %weight.1), channel_id=1, source_target_pairs={{0,1},{1,0},{2,3},{3,2},{4,5},{5,4},{6,7},{7,6},{8,9},{9,8},{10,11... | collective-permute-start | bytes 3145736 | tf_op jit(solution)/shard_map/ppermute | solution.py:281
  14.4 0.1 arrange.1._
  14.5 2.8 %all-to-all-done = bf16[8,8,512]{2,1,0:T(8,128)(2,1)S(1)} async-done(((bf16[8,8,512]{2,1,0:T(8,128)(2,1)}), bf16[8,8,512]{2,1,0:T(8,128)(2,1)S(1)}, u32[]{:S(2)}, u32[]{:S(2)}) %all-to-all-start) | async-done | bytes 65568 | tf_op jit(solution)/shard_map/all_to_all | solution.py:269
  17.3 0.0 collective-permute-done.peer
  17.3 0.0 copy-done
  17.3 0.0 copy-done.4
  17.3 0.0 copy-done.5
  17.3 0.0 copy-start.1
  17.3 0.0 copy-start.2
  17.3 0.0 copy-start.3
  17.3 4.3 %project.1 = (bf16[16,272,128]{2,1,0:T(8,128)(2,1)S(1)}, s32[80]{0:T(128)S(1)}) custom-call(s32[5]{0:T(128)S(1)} %copy-done.4, s32[64]{0:T(128)S(1)} %copy-done.5, bf16[64,512]{1,0:T(8,128)(2,1)S(1)} %bitcast.7, bf16[6208,256]{1,0:T(8,128)(2,1)S(1)} %bitcast.6, bf16[6208,256]{1,0:T(8,128)(2,1)} %collective-permute-done.peer, bf16[256,256]{1,0:T(8,128)(2,1)S(1)} %arrange.1._), custom_call_target="tpu_custom_call" | custom-call | tf_op jit(solution)/shard_map/project/pallas_call | solution.py:283
  21.7 0.0 collective-permute-done.1.swapped
  21.7 20.5 %all_to_all.20.received = bf16[16,272,128]{2,1,0:T(8,128)(2,1)S(1)} all-to-all(bf16[16,272,128]{2,1,0:T(8,128)(2,1)S(1)} %get-tuple-element.14), channel_id=1, replica_groups=mesh['dp'=32,'tensor'=16] {'tensor'}, dimensions={0} | all-to-all | bytes 2228224 | tf_op jit(solution)/shard_map/all_to_all | solution.py:296
  42.2 0.0 copy-done.1
  42.2 1.6 %mix.1 = (bf16[8,128,128]{2,1,0:T(8,128)(2,1)S(1)}, bf16[1024,256]{1,0:T(8,128)(2,1)S(1)}, bf16[1024,256]{1,0:T(8,128)(2,1)S(1)}) custom-call(s32[80]{0:T(128)S(1)} %get-tuple-element.12.plan_ref, f32[3,64]{1,0:T(4,128)S(1)} %copy-done.3, bf16[16,272,128]{2,1,0:T(8,128)(2,1)S(1)} %all_to_all.20.received, f32[4,4096]{1,0:T(4,128)S(1)} %copy-done.2, ...), custom_call_target="tpu_custom_call" | custom-call | tf_op jit(solution)/shard_map/mix/pallas_call | solution.py:298
  43.8 9.4 %all_to_all.21.gathered = bf16[8,128,128]{2,1,0:T(8,128)(2,1)S(1)} all-to-all(bf16[8,128,128]{2,1,0:T(8,128)(2,1)S(1)} %get-tuple-element.16), channel_id=1, replica_groups={{0,2,4,6,8,10,12,14},{1,3,5,7,9,11,13,15},{16,18,20,22,24,26,28,30},{17..., dimensions={0} | all-to-all | bytes 524288 | tf_op jit(solution)/shard_map/all_to_all | solution.py:317
  53.1 0.4 finish.1
  53.5 10.0 %all_to_all.22.received = bf16[16,8,512]{2,1,0:T(8,128)(2,1)S(1)} all-to-all(bf16[16,8,512]{2,1,0:T(8,128)(2,1)S(1)} %finish.1), channel_id=1, replica_groups=mesh['dp'=32,'tensor'=16] {'tensor'}, dimensions={0} | all-to-all | bytes 262144 | tf_op jit(solution)/shard_map/all_to_all | solution.py:329
  63.5 0.6 %combine.1 = bf16[8,4096]{1,0:T(8,128)(2,1)} custom-call(bf16[16,8,512]{2,1,0:T(8,128)(2,1)S(1)} %all_to_all.22.received), custom_call_target="tpu_custom_call" | custom-call | tf_op jit(solution)/shard_map/combine/pallas_call | solution.py:330
  (2 shorter events, 0.0 us)
Async XLA Ops:
  0.0 17.3 %collective-permute-start = (bf16[6208,256]{1,0:T(8,128)(2,1)}, bf16[6208,256]{1,0:T(8,128)(2,1)}, u32[]{:S(2)}, u32[]{:S(2)}) collective-permute-start(bf16[6208,256]{1,0:T(8,128)(2,1)} %bitcast.5), channel_id=1, source_target_pairs={{0,1},{1,0},{2,3},{3,2},{4,5},{5,4},{6,7},{7,6},{8,9},{9,8},{10,11... | collective-permute-start | bytes 9535496 | tf_op jit(solution)/shard_map/ppermute | solution.py:267
  8.8 8.5 %all-to-all-start = ((bf16[8,8,512]{2,1,0:T(8,128)(2,1)}), bf16[8,8,512]{2,1,0:T(8,128)(2,1)S(1)}, u32[]{:S(2)}, u32[]{:S(2)}) async-start(bf16[8,8,512]{2,1,0:T(8,128)(2,1)} %bitcast.8), calls=%async_computation | async-start | bytes 131072 | tf_op jit(solution)/shard_map/all_to_all | solution.py:269
  12.2 5.1 %copy-start = (bf16[256,6208]{0,1:T(8,128)(2,1)S(1)}, bf16[256,6208]{0,1:T(8,128)(2,1)}, u32[]{:S(2)}) copy-start(bf16[256,6208]{0,1:T(8,128)(2,1)} %param.8) | copy-start | bytes 9535492
  12.2 5.1 %copy-start.4 = (s32[5]{0:T(128)S(1)}, s32[5]{0:T(128)}, u32[]{:S(2)}) copy-start(s32[5]{0:T(128)} %packing.1) | copy-start | bytes 64
  12.2 5.1 %copy-start.5 = (s32[64]{0:T(128)S(1)}, s32[64]{0:T(128)}, u32[]{:S(2)}) copy-start(s32[64]{0:T(128)} %head_group.1) | copy-start | bytes 772
  12.2 9.5 %collective-permute-start.1 = (bf16[2048,256]{1,0:T(8,128)(2,1)}, bf16[2048,256]{1,0:T(8,128)(2,1)}, u32[]{:S(2)}, u32[]{:S(2)}) collective-permute-start(bf16[2048,256]{1,0:T(8,128)(2,1)} %weight.1), channel_id=1, source_target_pairs={{0,1},{1,0},{2,3},{3,2},{4,5},{5,4},{6,7},{7,6},{8,9},{9,8},{10,11... | collective-permute-start | bytes 3145736 | tf_op jit(solution)/shard_map/ppermute | solution.py:281
  17.3 24.9 %copy-start.1 = (bf16[2048,256]{1,0:T(8,128)(2,1)S(1)}, bf16[2048,256]{1,0:T(8,128)(2,1)}, u32[]{:S(2)}) copy-start(bf16[2048,256]{1,0:T(8,128)(2,1)} %weight.1) | copy-start | bytes 3145732
  17.3 24.9 %copy-start.2 = (f32[4,4096]{1,0:T(4,128)S(1)}, f32[4,4096]{1,0:T(4,128)}, u32[]{:S(2)}) copy-start(f32[4,4096]{1,0:T(4,128)} %taps_ref.1) | copy-start | bytes 196612
  17.3 24.9 %copy-start.3 = (f32[3,64]{1,0:T(4,128)S(1)}, f32[3,64]{1,0:T(4,128)}, u32[]{:S(2)}) copy-start(f32[3,64]{1,0:T(4,128)} %params_ref.1) | copy-start | bytes 2308

commit v6 on v5

--- a/solution.py
+++ b/solution.py
@@ -36,6 +36,7 @@
 CORE_SWAP = [(member, member ^ 1) for member in range(MEMBERS)]
 CHIP_GROUPS = [[2 * chip + core for chip in range(CHIPS)] for core in range(2)]
 ORDER, STARTS = 0, HEADS
+STREAMS = tuple((begin, min(1600, COLS - begin)) for begin in range(0, COLS, 1600))
 
 
 def arrange_kernel(arrange):
@@ -51,7 +52,24 @@
     return (2 * (member // 4) + member % 2) * 2 + (member // 2) % 2
 
 
-def project_kernel(packing, head_group, acts, own, peer, _, out, plan, steps_ref, sorted_ref):
+def project_kernel(
+    packing_ref, group_ref, acts, own, peer_ref, _, out, plan,
+    steps_ref, sorted_ref, peer, packing, head_group, arrived,
+):
+    scalars = [
+        pltpu.make_async_copy(packing_ref, packing, arrived.at[0]),
+        pltpu.make_async_copy(group_ref, head_group, arrived.at[1]),
+    ]
+    streams = [
+        pltpu.make_async_copy(
+            peer_ref.at[pl.ds(begin, extent), :], peer.at[pl.ds(begin, extent), :], arrived.at[2 + index]
+        )
+        for index, (begin, extent) in enumerate(STREAMS)
+    ]
+    for copy in (*scalars, *streams):
+        copy.start()
+    for copy in scalars:
+        copy.wait()
     begin = jnp.int32(0)
     for place in range(5):
         number = packing[place]
@@ -74,6 +92,8 @@
     )
     both = jnp.concatenate([both, both], axis=0).astype(F32).T.astype(BF16)
     low = lax.broadcasted_iota(jnp.int32, (CHANNELS, SEQ), 1) < HALF
+    for copy in streams:
+        copy.wait()
 
     def taken(number, begin, extent):
         where = pl.ds(pl.multiple_of(plan[STARTS + number] + begin, HEAD_DIM), extent)
@@ -286,9 +306,16 @@
             jax.ShapeDtypeStruct((MEMBERS, PACKED, SEQ), BF16),
             jax.ShapeDtypeStruct((80,), jnp.int32),
         ),
-        in_specs=[SMEM, SMEM, VMEM, VMEM, VMEM, pl.BlockSpec(memory_space=pl.ANY)],
+        in_specs=[ANY, ANY, VMEM, VMEM, ANY, ANY],
         out_specs=(VMEM, SMEM),
-        scratch_shapes=[pltpu.VMEM((HEADS, SEQ), F32), pltpu.VMEM((MEMBERS * DT_ROWS, SEQ), F32)],
+        scratch_shapes=[
+            pltpu.VMEM((HEADS, SEQ), F32),
+            pltpu.VMEM((MEMBERS * DT_ROWS, SEQ), F32),
+            pltpu.VMEM((COLS, ROWS), BF16),
+            pltpu.SMEM((5,), jnp.int32),
+            pltpu.SMEM((HEADS,), jnp.int32),
+            pltpu.SemaphoreType.DMA((2 + len(STREAMS),)),
+        ],
         compiler_params=pltpu.CompilerParams(vmem_limit_bytes=16 * 1024 * 1024),
         name="project",
     )(packing, head_group, acts, own, peer, arrange)

time: 64.5 us -> 64.2 us (level)
  no operation moved by 1% of the time
where the time goes in v6:
time: 64.2 us; the launch traced here: 63.9 us
  blocking collectives  39.8 us (62%)
  starting transfers between devices  14.3 us (22%)
  Pallas kernels  6.82 us (11%)
  waiting for transfers between devices  2.8 us (4%)
    all_to_all x1, blocking collectives, shards(): lax.all_to_all(partial, 'tensor', split_axis=0, concat_axis=0, tiled=True)  20.5 us
    all_to_all x1, blocking collectives, shards(): lax.all_to_all(share, 'tensor', split_axis=0, concat_axis=0, tiled=True)  9.96 us
    all_to_all x1, blocking collectives, shards(): lax.all_to_all(gated, 'tensor', split_axis=0, concat_axis=0, tiled=True,...  9.36 us
    ppermute x1, starting transfers between devices, shards(): peer = lax.ppermute(own, 'tensor', CORE_SWAP)  8.78 us
    pallas_call x1, Pallas kernels, shards(): pl.pallas_call(project_kernel, out_shape=(jax.ShapeDtypeStruct((MEMBERS,...  4.15 us
    all_to_all x1, starting transfers between devices, shards(): lax.all_to_all(per_chip, 'tensor', split_axis=0, concat_axis=0, tiled=Tru...  3.36 us
    all_to_all x1, waiting for transfers between devices, shards(): lax.all_to_all(per_chip, 'tensor', split_axis=0, concat_axis=0, tiled=Tru...  2.8 us
    ppermute x1, starting transfers between devices, shards(): swapped = lax.ppermute(out_weight, 'tensor', CORE_SWAP)  2.19 us
  transfers between devices with their start and end apart: 3, of which 1 were waited for; matrix products, arithmetic and copies ran while one was open for 0% of the time, Pallas kernels for 7%

profile of v6, /device:TPU:1, one launch (start us, length us, event | category | flops | bytes accessed | tf_op | source)
XLA Modules:
  0.0 63.9 jit_solution(10276107558382825373)
XLA Ops:
  0.0 8.8 %collective-permute-start = (bf16[6208,256]{1,0:T(8,128)(2,1)}, bf16[6208,256]{1,0:T(8,128)(2,1)}, u32[]{:S(2)}, u32[]{:S(2)}) collective-permute-start(bf16[6208,256]{1,0:T(8,128)(2,1)} %bitcast.5), channel_id=1, source_target_pairs={{0,1},{1,0},{2,3},{3,2},{4,5},{5,4},{6,7},{7,6},{8,9},{9,8},{10,11... | collective-permute-start | bytes 9535496 | tf_op jit(solution)/shard_map/ppermute | solution.py:287
  8.8 3.4 %all-to-all-start = ((bf16[8,8,512]{2,1,0:T(8,128)(2,1)}), bf16[8,8,512]{2,1,0:T(8,128)(2,1)S(1)}, u32[]{:S(2)}, u32[]{:S(2)}) async-start(bf16[8,8,512]{2,1,0:T(8,128)(2,1)} %bitcast.8), calls=%async_computation | async-start | bytes 131072 | tf_op jit(solution)/shard_map/all_to_all | solution.py:289
  12.2 0.0 copy-start
  12.2 0.0 copy-start.4
  12.2 0.0 copy-start.5
  12.2 2.2 %collective-permute-start.1 = (bf16[2048,256]{1,0:T(8,128)(2,1)}, bf16[2048,256]{1,0:T(8,128)(2,1)}, u32[]{:S(2)}, u32[]{:S(2)}) collective-permute-start(bf16[2048,256]{1,0:T(8,128)(2,1)} %weight.1), channel_id=1, source_target_pairs={{0,1},{1,0},{2,3},{3,2},{4,5},{5,4},{6,7},{7,6},{8,9},{9,8},{10,11... | collective-permute-start | bytes 3145736 | tf_op jit(solution)/shard_map/ppermute | solution.py:301
  14.4 0.1 arrange.1._
  14.5 2.8 %all-to-all-done = bf16[8,8,512]{2,1,0:T(8,128)(2,1)S(1)} async-done(((bf16[8,8,512]{2,1,0:T(8,128)(2,1)}), bf16[8,8,512]{2,1,0:T(8,128)(2,1)S(1)}, u32[]{:S(2)}, u32[]{:S(2)}) %all-to-all-start) | async-done | bytes 65568 | tf_op jit(solution)/shard_map/all_to_all | solution.py:289
  17.3 0.0 collective-permute-done.peer_ref
  17.3 0.0 copy-done
  17.3 0.0 copy-done.4
  17.3 0.0 copy-done.5
  17.3 0.0 copy-start.1
  17.3 0.0 copy-start.2
  17.3 0.0 copy-start.3
  17.3 4.1 %project.1 = (bf16[16,272,128]{2,1,0:T(8,128)(2,1)S(1)}, s32[80]{0:T(128)S(1)}) custom-call(s32[5]{0:T(128)S(1)} %copy-done.4, s32[64]{0:T(128)S(1)} %copy-done.5, bf16[64,512]{1,0:T(8,128)(2,1)S(1)} %bitcast.7, bf16[6208,256]{1,0:T(8,128)(2,1)S(1)} %bitcast.6, bf16[6208,256]{1,0:T(8,128)(2,1)} %collective-permute-done.peer_ref, bf16[256,256]{1,0:T(8,128)(2,1)S(1)} %arrange.1._), custom_call_target="tpu_custom_call" | custom-call | tf_op jit(solution)/shard_map/project/pallas_call | solution.py:303
  21.5 0.0 collective-permute-done.1.swapped
  21.5 20.5 %all_to_all.20.received = bf16[16,272,128]{2,1,0:T(8,128)(2,1)S(1)} all-to-all(bf16[16,272,128]{2,1,0:T(8,128)(2,1)S(1)} %get-tuple-element.14), channel_id=1, replica_groups=mesh['dp'=32,'tensor'=16] {'tensor'}, dimensions={0} | all-to-all | bytes 2228224 | tf_op jit(solution)/shard_map/all_to_all | solution.py:323
  42.0 0.0 copy-done.1
  42.0 1.6 %mix.1 = (bf16[8,128,128]{2,1,0:T(8,128)(2,1)S(1)}, bf16[1024,256]{1,0:T(8,128)(2,1)S(1)}, bf16[1024,256]{1,0:T(8,128)(2,1)S(1)}) custom-call(s32[80]{0:T(128)S(1)} %get-tuple-element.12.plan_ref, f32[3,64]{1,0:T(4,128)S(1)} %copy-done.3, bf16[16,272,128]{2,1,0:T(8,128)(2,1)S(1)} %all_to_all.20.received, f32[4,4096]{1,0:T(4,128)S(1)} %copy-done.2, ...), custom_call_target="tpu_custom_call" | custom-call | tf_op jit(solution)/shard_map/mix/pallas_call | solution.py:325
  43.6 9.4 %all_to_all.21.gathered = bf16[8,128,128]{2,1,0:T(8,128)(2,1)S(1)} all-to-all(bf16[8,128,128]{2,1,0:T(8,128)(2,1)S(1)} %get-tuple-element.16), channel_id=1, replica_groups={{0,2,4,6,8,10,12,14},{1,3,5,7,9,11,13,15},{16,18,20,22,24,26,28,30},{17..., dimensions={0} | all-to-all | bytes 524288 | tf_op jit(solution)/shard_map/all_to_all | solution.py:344
  52.9 0.4 finish.1
  53.3 10.0 %all_to_all.22.received = bf16[16,8,512]{2,1,0:T(8,128)(2,1)S(1)} all-to-all(bf16[16,8,512]{2,1,0:T(8,128)(2,1)S(1)} %finish.1), channel_id=1, replica_groups=mesh['dp'=32,'tensor'=16] {'tensor'}, dimensions={0} | all-to-all | bytes 262144 | tf_op jit(solution)/shard_map/all_to_all | solution.py:356
  63.3 0.6 %combine.1 = bf16[8,4096]{1,0:T(8,128)(2,1)} custom-call(bf16[16,8,512]{2,1,0:T(8,128)(2,1)S(1)} %all_to_all.22.received), custom_call_target="tpu_custom_call" | custom-call | tf_op jit(solution)/shard_map/combine/pallas_call | solution.py:357
  (2 shorter events, 0.0 us)
Async XLA Ops:
  0.0 17.3 %collective-permute-start = (bf16[6208,256]{1,0:T(8,128)(2,1)}, bf16[6208,256]{1,0:T(8,128)(2,1)}, u32[]{:S(2)}, u32[]{:S(2)}) collective-permute-start(bf16[6208,256]{1,0:T(8,128)(2,1)} %bitcast.5), channel_id=1, source_target_pairs={{0,1},{1,0},{2,3},{3,2},{4,5},{5,4},{6,7},{7,6},{8,9},{9,8},{10,11... | collective-permute-start | bytes 9535496 | tf_op jit(solution)/shard_map/ppermute | solution.py:287
  8.8 8.5 %all-to-all-start = ((bf16[8,8,512]{2,1,0:T(8,128)(2,1)}), bf16[8,8,512]{2,1,0:T(8,128)(2,1)S(1)}, u32[]{:S(2)}, u32[]{:S(2)}) async-start(bf16[8,8,512]{2,1,0:T(8,128)(2,1)} %bitcast.8), calls=%async_computation | async-start | bytes 131072 | tf_op jit(solution)/shard_map/all_to_all | solution.py:289
  12.2 5.1 %copy-start = (bf16[256,6208]{0,1:T(8,128)(2,1)S(1)}, bf16[256,6208]{0,1:T(8,128)(2,1)}, u32[]{:S(2)}) copy-start(bf16[256,6208]{0,1:T(8,128)(2,1)} %param.8) | copy-start | bytes 9535492
  12.2 5.1 %copy-start.4 = (s32[5]{0:T(128)S(1)}, s32[5]{0:T(128)}, u32[]{:S(2)}) copy-start(s32[5]{0:T(128)} %packing_ref.1) | copy-start | bytes 64
  12.2 5.1 %copy-start.5 = (s32[64]{0:T(128)S(1)}, s32[64]{0:T(128)}, u32[]{:S(2)}) copy-start(s32[64]{0:T(128)} %group_ref.1) | copy-start | bytes 772
  12.2 9.3 %collective-permute-start.1 = (bf16[2048,256]{1,0:T(8,128)(2,1)}, bf16[2048,256]{1,0:T(8,128)(2,1)}, u32[]{:S(2)}, u32[]{:S(2)}) collective-permute-start(bf16[2048,256]{1,0:T(8,128)(2,1)} %weight.1), channel_id=1, source_target_pairs={{0,1},{1,0},{2,3},{3,2},{4,5},{5,4},{6,7},{7,6},{8,9},{9,8},{10,11... | collective-permute-start | bytes 3145736 | tf_op jit(solution)/shard_map/ppermute | solution.py:301
  17.3 24.7 %copy-start.1 = (bf16[2048,256]{1,0:T(8,128)(2,1)S(1)}, bf16[2048,256]{1,0:T(8,128)(2,1)}, u32[]{:S(2)}) copy-start(bf16[2048,256]{1,0:T(8,128)(2,1)} %weight.1) | copy-start | bytes 3145732
  17.3 24.7 %copy-start.2 = (f32[4,4096]{1,0:T(4,128)S(1)}, f32[4,4096]{1,0:T(4,128)}, u32[]{:S(2)}) copy-start(f32[4,4096]{1,0:T(4,128)} %taps_ref.1) | copy-start | bytes 196612
  17.3 24.7 %copy-start.3 = (f32[3,64]{1,0:T(4,128)S(1)}, f32[3,64]{1,0:T(4,128)}, u32[]{:S(2)}) copy-start(f32[3,64]{1,0:T(4,128)} %params_ref.1) | copy-start | bytes 2308

commit v7 on v6

--- a/solution.py
+++ b/solution.py
@@ -36,7 +36,7 @@
 CORE_SWAP = [(member, member ^ 1) for member in range(MEMBERS)]
 CHIP_GROUPS = [[2 * chip + core for chip in range(CHIPS)] for core in range(2)]
 ORDER, STARTS = 0, HEADS
-STREAMS = tuple((begin, min(1600, COLS - begin)) for begin in range(0, COLS, 1600))
+STREAMS = tuple((begin, min(800, COLS - begin)) for begin in range(0, COLS, 800))
 
 
 def arrange_kernel(arrange):

time: 64.2 us -> 64.3 us (level)
  no operation moved by 1% of the time
where the time goes in v7:
time: 64.3 us; the launch traced here: 63.9 us
  blocking collectives  39.8 us (62%)
  starting transfers between devices  14.3 us (22%)
  Pallas kernels  6.84 us (11%)
  waiting for transfers between devices  2.8 us (4%)
    all_to_all x1, blocking collectives, shards(): lax.all_to_all(partial, 'tensor', split_axis=0, concat_axis=0, tiled=True)  20.5 us
    all_to_all x1, blocking collectives, shards(): lax.all_to_all(share, 'tensor', split_axis=0, concat_axis=0, tiled=True)  9.96 us
    all_to_all x1, blocking collectives, shards(): lax.all_to_all(gated, 'tensor', split_axis=0, concat_axis=0, tiled=True,...  9.35 us
    ppermute x1, starting transfers between devices, shards(): peer = lax.ppermute(own, 'tensor', CORE_SWAP)  8.78 us
    pallas_call x1, Pallas kernels, shards(): pl.pallas_call(project_kernel, out_shape=(jax.ShapeDtypeStruct((MEMBERS,...  4.16 us
    all_to_all x1, starting transfers between devices, shards(): lax.all_to_all(per_chip, 'tensor', split_axis=0, concat_axis=0, tiled=Tru...  3.36 us
    all_to_all x1, waiting for transfers between devices, shards(): lax.all_to_all(per_chip, 'tensor', split_axis=0, concat_axis=0, tiled=Tru...  2.8 us
    ppermute x1, starting transfers between devices, shards(): swapped = lax.ppermute(out_weight, 'tensor', CORE_SWAP)  2.19 us
  transfers between devices with their start and end apart: 3, of which 1 were waited for; matrix products, arithmetic and copies ran while one was open for 0% of the time, Pallas kernels for 7%

profile of v7, /device:TPU:1, one launch (start us, length us, event | category | flops | bytes accessed | tf_op | source)
XLA Modules:
  0.0 63.9 jit_solution(13647503822285608263)
XLA Ops:
  0.0 8.8 %collective-permute-start = (bf16[6208,256]{1,0:T(8,128)(2,1)}, bf16[6208,256]{1,0:T(8,128)(2,1)}, u32[]{:S(2)}, u32[]{:S(2)}) collective-permute-start(bf16[6208,256]{1,0:T(8,128)(2,1)} %bitcast.5), channel_id=1, source_target_pairs={{0,1},{1,0},{2,3},{3,2},{4,5},{5,4},{6,7},{7,6},{8,9},{9,8},{10,11... | collective-permute-start | bytes 9535496 | tf_op jit(solution)/shard_map/ppermute | solution.py:287
  8.8 3.4 %all-to-all-start = ((bf16[8,8,512]{2,1,0:T(8,128)(2,1)}), bf16[8,8,512]{2,1,0:T(8,128)(2,1)S(1)}, u32[]{:S(2)}, u32[]{:S(2)}) async-start(bf16[8,8,512]{2,1,0:T(8,128)(2,1)} %bitcast.8), calls=%async_computation | async-start | bytes 131072 | tf_op jit(solution)/shard_map/all_to_all | solution.py:289
  12.2 0.0 copy-start
  12.2 0.0 copy-start.4
  12.2 0.0 copy-start.5
  12.2 2.2 %collective-permute-start.1 = (bf16[2048,256]{1,0:T(8,128)(2,1)}, bf16[2048,256]{1,0:T(8,128)(2,1)}, u32[]{:S(2)}, u32[]{:S(2)}) collective-permute-start(bf16[2048,256]{1,0:T(8,128)(2,1)} %weight.1), channel_id=1, source_target_pairs={{0,1},{1,0},{2,3},{3,2},{4,5},{5,4},{6,7},{7,6},{8,9},{9,8},{10,11... | collective-permute-start | bytes 3145736 | tf_op jit(solution)/shard_map/ppermute | solution.py:301
  14.4 0.1 arrange.1._
  14.5 2.8 %all-to-all-done = bf16[8,8,512]{2,1,0:T(8,128)(2,1)S(1)} async-done(((bf16[8,8,512]{2,1,0:T(8,128)(2,1)}), bf16[8,8,512]{2,1,0:T(8,128)(2,1)S(1)}, u32[]{:S(2)}, u32[]{:S(2)}) %all-to-all-start) | async-done | bytes 65568 | tf_op jit(solution)/shard_map/all_to_all | solution.py:289
  17.3 0.0 collective-permute-done.peer_ref
  17.3 0.0 copy-done
  17.3 0.0 copy-done.4
  17.3 0.0 copy-done.5
  17.3 0.0 copy-start.1
  17.3 0.0 copy-start.2
  17.3 0.0 copy-start.3
  17.3 4.2 %project.1 = (bf16[16,272,128]{2,1,0:T(8,128)(2,1)S(1)}, s32[80]{0:T(128)S(1)}) custom-call(s32[5]{0:T(128)S(1)} %copy-done.4, s32[64]{0:T(128)S(1)} %copy-done.5, bf16[64,512]{1,0:T(8,128)(2,1)S(1)} %bitcast.7, bf16[6208,256]{1,0:T(8,128)(2,1)S(1)} %bitcast.6, bf16[6208,256]{1,0:T(8,128)(2,1)} %collective-permute-done.peer_ref, bf16[256,256]{1,0:T(8,128)(2,1)S(1)} %arrange.1._), custom_call_target="tpu_custom_call" | custom-call | tf_op jit(solution)/shard_map/project/pallas_call | solution.py:303
  21.5 0.0 collective-permute-done.1.swapped
  21.5 20.5 %all_to_all.20.received = bf16[16,272,128]{2,1,0:T(8,128)(2,1)S(1)} all-to-all(bf16[16,272,128]{2,1,0:T(8,128)(2,1)S(1)} %get-tuple-element.14), channel_id=1, replica_groups=mesh['dp'=32,'tensor'=16] {'tensor'}, dimensions={0} | all-to-all | bytes 2228224 | tf_op jit(solution)/shard_map/all_to_all | solution.py:323
  42.0 0.0 copy-done.2
  42.0 1.6 %mix.1 = (bf16[8,128,128]{2,1,0:T(8,128)(2,1)S(1)}, bf16[1024,256]{1,0:T(8,128)(2,1)S(1)}, bf16[1024,256]{1,0:T(8,128)(2,1)S(1)}) custom-call(s32[80]{0:T(128)S(1)} %get-tuple-element.12.plan_ref, f32[3,64]{1,0:T(4,128)S(1)} %copy-done.3, bf16[16,272,128]{2,1,0:T(8,128)(2,1)S(1)} %all_to_all.20.received, f32[4,4096]{1,0:T(4,128)S(1)} %copy-done.2, ...), custom_call_target="tpu_custom_call" | custom-call | tf_op jit(solution)/shard_map/mix/pallas_call | solution.py:325
  43.6 9.4 %all_to_all.21.gathered = bf16[8,128,128]{2,1,0:T(8,128)(2,1)S(1)} all-to-all(bf16[8,128,128]{2,1,0:T(8,128)(2,1)S(1)} %get-tuple-element.16), channel_id=1, replica_groups={{0,2,4,6,8,10,12,14},{1,3,5,7,9,11,13,15},{16,18,20,22,24,26,28,30},{17..., dimensions={0} | all-to-all | bytes 524288 | tf_op jit(solution)/shard_map/all_to_all | solution.py:344
  53.0 0.4 finish.1
  53.3 10.0 %all_to_all.22.received = bf16[16,8,512]{2,1,0:T(8,128)(2,1)S(1)} all-to-all(bf16[16,8,512]{2,1,0:T(8,128)(2,1)S(1)} %finish.1), channel_id=1, replica_groups=mesh['dp'=32,'tensor'=16] {'tensor'}, dimensions={0} | all-to-all | bytes 262144 | tf_op jit(solution)/shard_map/all_to_all | solution.py:356
  63.3 0.6 %combine.1 = bf16[8,4096]{1,0:T(8,128)(2,1)} custom-call(bf16[16,8,512]{2,1,0:T(8,128)(2,1)S(1)} %all_to_all.22.received), custom_call_target="tpu_custom_call" | custom-call | tf_op jit(solution)/shard_map/combine/pallas_call | solution.py:357
  (2 shorter events, 0.0 us)
Async XLA Ops:
  0.0 17.3 %collective-permute-start = (bf16[6208,256]{1,0:T(8,128)(2,1)}, bf16[6208,256]{1,0:T(8,128)(2,1)}, u32[]{:S(2)}, u32[]{:S(2)}) collective-permute-start(bf16[6208,256]{1,0:T(8,128)(2,1)} %bitcast.5), channel_id=1, source_target_pairs={{0,1},{1,0},{2,3},{3,2},{4,5},{5,4},{6,7},{7,6},{8,9},{9,8},{10,11... | collective-permute-start | bytes 9535496 | tf_op jit(solution)/shard_map/ppermute | solution.py:287
  8.8 8.5 %all-to-all-start = ((bf16[8,8,512]{2,1,0:T(8,128)(2,1)}), bf16[8,8,512]{2,1,0:T(8,128)(2,1)S(1)}, u32[]{:S(2)}, u32[]{:S(2)}) async-start(bf16[8,8,512]{2,1,0:T(8,128)(2,1)} %bitcast.8), calls=%async_computation | async-start | bytes 131072 | tf_op jit(solution)/shard_map/all_to_all | solution.py:289
  12.2 5.1 %copy-start = (bf16[256,6208]{0,1:T(8,128)(2,1)S(1)}, bf16[256,6208]{0,1:T(8,128)(2,1)}, u32[]{:S(2)}) copy-start(bf16[256,6208]{0,1:T(8,128)(2,1)} %param.8) | copy-start | bytes 9535492
  12.2 5.1 %copy-start.4 = (s32[5]{0:T(128)S(1)}, s32[5]{0:T(128)}, u32[]{:S(2)}) copy-start(s32[5]{0:T(128)} %packing_ref.1) | copy-start | bytes 64
  12.2 5.1 %copy-start.5 = (s32[64]{0:T(128)S(1)}, s32[64]{0:T(128)}, u32[]{:S(2)}) copy-start(s32[64]{0:T(128)} %group_ref.1) | copy-start | bytes 772
  12.2 9.3 %collective-permute-start.1 = (bf16[2048,256]{1,0:T(8,128)(2,1)}, bf16[2048,256]{1,0:T(8,128)(2,1)}, u32[]{:S(2)}, u32[]{:S(2)}) collective-permute-start(bf16[2048,256]{1,0:T(8,128)(2,1)} %weight.1), channel_id=1, source_target_pairs={{0,1},{1,0},{2,3},{3,2},{4,5},{5,4},{6,7},{7,6},{8,9},{9,8},{10,11... | collective-permute-start | bytes 3145736 | tf_op jit(solution)/shard_map/ppermute | solution.py:301
  17.3 24.7 %copy-start.1 = (bf16[2048,256]{1,0:T(8,128)(2,1)S(1)}, bf16[2048,256]{1,0:T(8,128)(2,1)}, u32[]{:S(2)}) copy-start(bf16[2048,256]{1,0:T(8,128)(2,1)} %weight.1) | copy-start | bytes 3145732
  17.3 24.7 %copy-start.2 = (f32[4,4096]{1,0:T(4,128)S(1)}, f32[4,4096]{1,0:T(4,128)}, u32[]{:S(2)}) copy-start(f32[4,4096]{1,0:T(4,128)} %taps_ref.1) | copy-start | bytes 196612
  17.3 24.7 %copy-start.3 = (f32[3,64]{1,0:T(4,128)S(1)}, f32[3,64]{1,0:T(4,128)}, u32[]{:S(2)}) copy-start(f32[3,64]{1,0:T(4,128)} %params_ref.1) | copy-start | bytes 2308
